TPU v7x, 32 devices: a whole 2x2x4 slice. The times are simulated.
32 devices in a mesh: grp: 2 (over x), row: 16 (over z, y, core).
Axes of the slice: x: 2, y: 2, z: 4, core: 2. Of those that a mesh axis runs over, the one named last changes fastest.
Arguments:
- facet_rows: bfloat16 [2, 16, 1024, 128], P(None, None, ('grp', 'row')), parts along dimension 2, may hold values from -6 to 6
- range_start: int32 [64], P('grp'), parts along dimension 0, may hold values from 0 to 511, as said below
- range_length: int32 [64], P('grp'), parts along dimension 0, may hold values from 128 to 256, as said below
- facet_offset: int32 [32], P('grp'), parts along dimension 0, may hold values from 0 to 511
- window_table: float32 [16, 256], replicated, may hold values from 0.25 to 1
- kernel_table: float32 [256, 8], replicated, may hold values from 0.05 to 0.5
- cell_row: int32 [64, 8192], P(('grp', 'row')), parts along dimension 0, may hold values from 0 to 248
- cell_column: int32 [64, 8192], P(('grp', 'row')), parts along dimension 0, may hold values from 0 to 248
- kernel_row: int32 [64, 8192], P(('grp', 'row')), parts along dimension 0, may hold values from 0 to 255
- kernel_column: int32 [64, 8192], P(('grp', 'row')), parts along dimension 0, may hold values from 0 to 255
Outputs:
- visibilities: float32 [2, 64, 8192], P(None, 'grp', 'row'), parts along dimension 1
There are 2 independent parts, one for each index of `grp`. A program takes and returns all parts, laid end to end along the dimension named above; an argument that names none is the same for every part. Nothing has to cross between parts.
Inputs may be any that keep to these rules, and one draw needn't show every extreme that they name: Subgrid s is held by row index e = s // 2; its range, range_start[s] to range_start[s] + range_length[s] - 1 taken modulo 512, lies within u from e * 32 - 256 // 2 to (e + 1) * 32 + 256 // 2 - 1 modulo 512. `range_length`: ranges of uneven length.
All inputs are finite; a program needn't handle non-finite values.
Results may differ from a plain program's by a relative error of at most 0.0057.
Values may be sent and summed in bfloat16 or wider, within the bound.
No kernel may reach another device: no remote copies, remote signals or barrier semaphores. Data moves between devices by JAX's collectives and lax.ppermute only.
A program may use at most 64 MiB of HBM per device.

v0:
```python
import math

import jax
import jax.numpy as jnp
import numpy as np
from jax import lax
from jax.experimental import pallas as pl
from jax.experimental.pallas import tpu as pltpu
from jax.sharding import PartitionSpec as P

F = 16
KC = 128
SUB = 256
R_DEV = 32
SUB_DEV = 2
SUPPORT = 8
NOVER = 256
CHIP = 2 * R_DEV
LANES = 128

TWO_PI = 2.0 * math.pi

VMEM = pl.BlockSpec(memory_space=pltpu.VMEM)
SMEM = pl.BlockSpec(memory_space=pltpu.SMEM)


def transform_table():
    kcol = np.arange(KC)
    jcol = np.arange(SUB)
    angles = np.float32(TWO_PI) * (kcol[:, None] * jcol[None, :] % SUB).astype(np.float32) / np.float32(SUB)
    scale = np.float32(1.0 / math.sqrt(KC))
    real_part = (np.cos(angles) * scale).astype(jnp.bfloat16)
    imag_part = (np.sin(angles) * scale).astype(jnp.bfloat16)
    upper = np.concatenate([real_part, imag_part], axis=1)
    lower = np.concatenate([-imag_part, real_part], axis=1)
    return np.ascontiguousarray(np.concatenate([upper, lower], axis=0).T)


def partners(chip, chips):
    return [
        chip ^ 1,
        (((chip + 1) ^ 1) + chips - 1) % chips,
        chip ^ 2,
        (((chip + 2) ^ 2) + chips - 2) % chips,
    ]


def facet_kernel(
    devices,
    start_ref,
    length_ref,
    offset_ref,
    window_ref,
    own_ref,
    other_ref,
    *rest,
):
    outs, padded = rest[:5], rest[5]
    total_rows = devices * R_DEV
    chips = devices // 2
    position = lax.axis_index("row")
    chip = position // 2
    core = position % 2
    padded[:R_DEV, :] = jnp.zeros((R_DEV, F), jnp.float32)
    padded[R_DEV + SUB :, :] = jnp.zeros((R_DEV, F), jnp.float32)
    padded[R_DEV : R_DEV + SUB, :] = jnp.transpose(window_ref[...])
    targets = [chip] + partners(chip, chips)
    row_index = lax.broadcasted_iota(jnp.int32, (R_DEV, F), 0)
    for held, source in enumerate((own_ref, other_ref)):
        half = core if held == 0 else 1 - core
        base = chip * CHIP + half * R_DEV
        turns = (offset_ref[...] * (base + row_index)) & (total_rows - 1)
        angles = TWO_PI * turns.astype(jnp.float32) / total_rows
        cosines = jnp.cos(angles)
        sines = jnp.sin(angles)
        weights = []
        for target in targets:
            for sub in range(SUB_DEV):
                subgrid = (target * 2 + core) * SUB_DEV + sub
                slot = (base - start_ref[subgrid]) & (total_rows - 1)
                slot = jnp.where(slot > total_rows - R_DEV, slot - total_rows, slot)
                slot = jnp.minimum(slot, SUB)
                piece = padded[pl.ds(slot + R_DEV, R_DEV), :]
                weights.append(jnp.where(slot + row_index < length_ref[subgrid], piece, 0.0))
        for tile in range(R_DEV // 16):
            rows = slice(16 * tile, 16 * tile + 16)
            sums = [[None, None] for _ in weights]
            for f in range(F):
                real_in = source[0, f, rows, :].astype(jnp.float32)
                imag_in = source[1, f, rows, :].astype(jnp.float32)
                cos_f = cosines[rows, f : f + 1]
                sin_f = sines[rows, f : f + 1]
                real_part = cos_f * real_in - sin_f * imag_in
                imag_part = cos_f * imag_in + sin_f * real_in
                for entry, weight in zip(sums, weights):
                    w = jnp.broadcast_to(weight[rows, f : f + 1], (16, KC))
                    entry[0] = w * real_part if f == 0 else entry[0] + w * real_part
                    entry[1] = w * imag_part if f == 0 else entry[1] + w * imag_part
            for place, entry in enumerate(sums):
                first = pl.multiple_of((place % SUB_DEV) * CHIP + half * R_DEV + 16 * tile, 16)
                out = outs[place // SUB_DEV]
                out[pl.ds(first, 16), :KC] = entry[0].astype(jnp.bfloat16)
                out[pl.ds(first, 16), KC:] = entry[1].astype(jnp.bfloat16)


def taps(low, high, cell, table_row):
    count = cell.shape[1]
    cell = jnp.broadcast_to(cell, (SUPPORT, count))
    table_row = jnp.broadcast_to(table_row, (SUPPORT, count))
    place = table_row & (LANES - 1)
    picked = []
    for first in range(0, count, LANES):
        index = place[:, first : first + LANES]
        from_low = jnp.take_along_axis(low, index, axis=1, mode="promise_in_bounds")
        from_high = jnp.take_along_axis(high, index, axis=1, mode="promise_in_bounds")
        picked.append(jnp.where(table_row[:, first : first + LANES] < LANES, from_low, from_high))
    weights = jnp.concatenate(picked, axis=1)
    for bit in range(3):
        turned = pltpu.roll(weights, 1 << bit, axis=0)
        weights = jnp.where((cell & (1 << bit)) != 0, turned, weights)
    sublane = lax.broadcasted_iota(jnp.int32, (SUPPORT, count), 0)
    tile = (cell >> 3) + jnp.where(sublane < (cell & 7), 1, 0)
    return weights, tile


def degrid_kernel(
    devices,
    per_dest,
    start_ref,
    table_ref,
    transform_ref,
    own_ref,
    first_ref,
    second_ref,
    third_ref,
    fourth_ref,
    row_ref,
    column_ref,
    row_kernel_ref,
    column_kernel_ref,
    out_ref,
    cells,
    gathered,
):
    position = lax.axis_index("row")
    chip = position // 2
    even = chip % 2 == 0
    table = jnp.transpose(table_ref[...])
    near = table.astype(jnp.bfloat16).astype(jnp.float32)
    near_low, near_high = near[:, :LANES], near[:, LANES:]
    table_low, table_high = table[:, :LANES], table[:, LANES:]
    for sub in range(SUB_DEV):
        rows = slice(sub * CHIP, sub * CHIP + CHIP)
        first, second = first_ref[rows, :], second_ref[rows, :]
        summed = jnp.concatenate(
            [
                own_ref[rows, :],
                jnp.where(even, first, second),
                third_ref[rows, :] + fourth_ref[rows, :],
                jnp.where(even, second, first),
            ],
            axis=0,
        )
        cells[sub] = lax.dot_general(
            transform_ref[...], summed, (((1,), (1,)), ((), ())), preferred_element_type=jnp.float32
        ).astype(jnp.bfloat16)

    def one_dest(dest, carry):
        lanes = pl.ds(pl.multiple_of(dest * per_dest, per_dest), per_dest)
        for sub in range(SUB_DEV):
            subgrid = position * SUB_DEV + sub
            shift = start_ref[subgrid] - chip * CHIP
            cell_row = (row_ref[sub : sub + 1, lanes] + shift) & (SUB - 1)
            weights, tile = taps(near_low, near_high, cell_row, row_kernel_ref[sub : sub + 1, lanes])
            tile = tile & (SUB // 8 - 1)
            odd = (tile & 1) != 0
            pair = (tile >> 1).astype(jnp.float32)
            pairs = jnp.concatenate(
                [jnp.where(odd, -1.0, pair), jnp.where(odd, pair, -1.0)], axis=0
            ).astype(jnp.bfloat16)
            both = jnp.concatenate([weights, weights], axis=0).astype(jnp.bfloat16)
            zero = jnp.zeros_like(both)
            spread = jnp.concatenate(
                [jnp.where(pairs == jnp.bfloat16(t), both, zero) for t in range(SUB // 16)], axis=0
            )
            along = jnp.dot(cells[sub], spread, preferred_element_type=jnp.float32)
            weights, tile = taps(
                table_low, table_high, column_ref[sub : sub + 1, lanes], column_kernel_ref[sub : sub + 1, lanes]
            )
            real_part = along[:8]
            imag_part = along[SUB : SUB + 8]
            for t in range(1, SUB // 8):
                here = tile == t
                real_part = jnp.where(here, along[8 * t : 8 * t + 8], real_part)
                imag_part = jnp.where(here, along[SUB + 8 * t : SUB + 8 * t + 8], imag_part)
            sums = [
                jnp.sum(weights * real_part, axis=0, keepdims=True),
                jnp.sum(weights * imag_part, axis=0, keepdims=True),
            ]
            chunks = per_dest // LANES
            for part in range(2):
                for chunk in range(chunks):
                    gathered[pl.ds(dest * 4 * chunks + (sub * 2 + part) * chunks + chunk, 1), :] = sums[part][
                        :, chunk * LANES : (chunk + 1) * LANES
                    ]
        return carry

    lax.fori_loop(0, devices, one_dest, 0)
    out_ref[...] = gathered[...].astype(jnp.bfloat16)


def place_kernel(devices, chunks, in_ref, out_ref, wide):
    wide[...] = in_ref[...].astype(jnp.float32)
    for part in range(2):
        for chunk in range(chunks):
            out_ref[part, :, chunk * LANES : (chunk + 1) * LANES] = wide[
                pl.ds(part * chunks + chunk, devices * SUB_DEV, stride=2 * chunks), :
            ]


def local(
    facet_rows,
    range_start,
    range_length,
    facet_offset,
    window_table,
    kernel_table,
    cell_row,
    cell_column,
    kernel_row,
    kernel_column,
):
    devices = lax.axis_size("row")
    chips = devices // 2
    slots = cell_row.shape[1]
    per_dest = slots // devices
    chunks = per_dest // LANES
    other_rows = lax.ppermute(facet_rows, "row", [(i, i ^ 1) for i in range(devices)])
    piece = jax.ShapeDtypeStruct((SUB_DEV * CHIP, 2 * KC), jnp.bfloat16)
    pieces = pl.pallas_call(
        lambda *refs: facet_kernel(devices, *refs),
        out_shape=[piece] * 5,
        in_specs=[SMEM, SMEM, VMEM, VMEM, VMEM, VMEM],
        out_specs=[VMEM] * 5,
        scratch_shapes=[pltpu.VMEM((SUB + 2 * R_DEV, F), jnp.float32)],
        name="facet_sums",
    )(range_start, range_length, facet_offset.reshape(1, F), window_table, facet_rows, other_rows)
    came = []
    for pairing in range(4):
        pairs = [
            (2 * chip + core, 2 * partners(chip, chips)[pairing] + core)
            for chip in range(chips)
            for core in range(2)
        ]
        came.append(lax.ppermute(pieces[1 + pairing], "row", pairs))
    rows_out = devices * 4 * chunks
    results = pl.pallas_call(
        lambda *refs: degrid_kernel(devices, per_dest, *refs),
        out_shape=jax.ShapeDtypeStruct((rows_out, LANES), jnp.bfloat16),
        in_specs=[SMEM] + [VMEM] * 11,
        out_specs=VMEM,
        scratch_shapes=[
            pltpu.VMEM((SUB_DEV, 2 * SUB, SUB), jnp.bfloat16),
            pltpu.VMEM((rows_out, LANES), jnp.float32),
        ],
        compiler_params=pltpu.CompilerParams(vmem_limit_bytes=32 * 1024 * 1024),
        name="degrid",
    )(
        range_start,
        kernel_table,
        jnp.asarray(transform_table()),
        pieces[0],
        *came,
        cell_row,
        cell_column,
        kernel_row,
        kernel_column,
    )
    received = lax.all_to_all(
        results.reshape(devices, 4 * chunks, LANES), "row", split_axis=0, concat_axis=0, tiled=True
    )
    return pl.pallas_call(
        lambda *refs: place_kernel(devices, chunks, *refs),
        out_shape=jax.ShapeDtypeStruct((2, devices * SUB_DEV, per_dest), jnp.float32),
        in_specs=[VMEM],
        out_specs=VMEM,
        scratch_shapes=[pltpu.VMEM((rows_out, LANES), jnp.float32)],
        name="place",
    )(received.reshape(rows_out, LANES))


def solution(mesh):
    placed = (
        P(None, None, ("grp", "row"), None),
        P("grp"),
        P("grp"),
        P("grp"),
        P(),
        P(),
        P(("grp", "row"), None),
        P(("grp", "row"), None),
        P(("grp", "row"), None),
        P(("grp", "row"), None),
    )
    return jax.shard_map(
        local, mesh=mesh, in_specs=placed, out_specs=P(None, "grp", "row"), check_vma=False
    )
```

profile of v0, /device:TPU:0, one launch (start us, length us, event | category | flops | bytes accessed | tf_op | source)
XLA Modules:
  0.0 42.3 jit_solution(4534893692593701172)
XLA Ops:
  0.0 0.5 %collective-permute-start = (bf16[2,16,32,128]{3,2,1,0:T(8,128)(2,1)}, bf16[2,16,32,128]{3,2,1,0:T(8,128)(2,1)S(1)}, u32[]{:S(2)}, u32[]{:S(2)}) collective-permute-start(bf16[2,16,32,128]{3,2,1,0:T(8,128)(2,1)} %refs_4_.1), channel_id=1, source_target_pairs={{0,1},{1,0},{2,3},{3,2},{4,5},{5,4},{6,7},{7,6},{8,9},{9,8},{10,11... | collective-permute-start | bytes 786440 | tf_op jit(solution)/shard_map/ppermute | solution.py:238
  0.5 1.4 %collective-permute-done.refs_5_ = bf16[2,16,32,128]{3,2,1,0:T(8,128)(2,1)S(1)} collective-permute-done((bf16[2,16,32,128]{3,2,1,0:T(8,128)(2,1)}, bf16[2,16,32,128]{3,2,1,0:T(8,128)(2,1)S(1)}, u32[]{:S(2)}, u32[]{:S(2)}) %collective-permute-start) | collective-permute-done | bytes 262176 | tf_op jit(solution)/shard_map/ppermute | solution.py:238
  1.8 0.0 copy-start.7
  1.8 0.7 %copy-done.7 = bf16[2,16,32,128]{3,2,1,0:T(8,128)(2,1)} copy-done((bf16[2,16,32,128]{3,2,1,0:T(8,128)(2,1)}, bf16[2,16,32,128]{3,2,1,0:T(8,128)(2,1)S(1)}, u32[]{:S(2)}) %copy-start.7) | copy-done | bytes 262168
  2.5 0.0 copy-start.8
  2.5 0.0 copy-start
  2.5 0.0 copy-start.3
  2.5 0.0 copy-start.4
  2.5 3.9 %facet_sums.1 = (bf16[128,256]{1,0:T(8,128)(2,1)}, bf16[128,256]{1,0:T(8,128)(2,1)}, bf16[128,256]{1,0:T(8,128)(2,1)}, bf16[128,256]{1,0:T(8,128)(2,1)}, bf16[128,256]{1,0:T(8,128)(2,1)}) custom-call(s32[32]{0:T(128)} %refs_0_.3, s32[32]{0:T(128)} %refs_1_.2, s32[1,16]{1,0:T(1,128)} %bitcast.5, f32[16,256]{1,0:T(8,128)} %refs_3_.1, ...), custom_call_target="tpu_custom_call" | custom-call | tf_op jit(solution)/shard_map/facet_sums/pallas_call | solution.py:240
  6.5 2.9 %collective-permute-start.1 = (bf16[128,256]{1,0:T(8,128)(2,1)}, bf16[128,256]{1,0:T(8,128)(2,1)S(1)}, u32[]{:S(2)}, u32[]{:S(2)}) collective-permute-start(bf16[128,256]{1,0:T(8,128)(2,1)} %get-tuple-element.11), channel_id=1, source_target_pairs={{0,2},{1,3},{2,0},{3,1},{4,6},{5,7},{6,4},{7,5},{8,10},{9,11},{10,... | collective-permute-start | bytes 196616 | tf_op jit(solution)/shard_map/ppermute | solution.py:255
  9.4 3.5 %collective-permute-start.2 = (bf16[128,256]{1,0:T(8,128)(2,1)}, bf16[128,256]{1,0:T(8,128)(2,1)S(1)}, u32[]{:S(2)}, u32[]{:S(2)}) collective-permute-start(bf16[128,256]{1,0:T(8,128)(2,1)} %get-tuple-element.12), channel_id=1, source_target_pairs={{0,14},{1,15},{2,4},{3,5},{4,2},{5,3},{6,8},{7,9},{8,6},{9,7},{10,... | collective-permute-start | bytes 196616 | tf_op jit(solution)/shard_map/ppermute | solution.py:255
  12.9 0.0 collective-permute-start.3
  12.9 0.0 copy-start.1
  12.9 0.9 %collective-permute-start.4 = (bf16[128,256]{1,0:T(8,128)(2,1)}, bf16[128,256]{1,0:T(8,128)(2,1)S(1)}, u32[]{:S(2)}, u32[]{:S(2)}) collective-permute-start(bf16[128,256]{1,0:T(8,128)(2,1)} %get-tuple-element.14), channel_id=1, source_target_pairs={{0,12},{1,13},{2,14},{3,15},{4,8},{5,9},{6,10},{7,11},{8,4},{9,5},... | collective-permute-start | bytes 196616 | tf_op jit(solution)/shard_map/ppermute | solution.py:255
  13.8 0.0 copy-done.8
  13.8 0.1 copy.12.refs_1_
  13.9 0.0 copy-start.6
  14.0 0.0 collective-permute-done.1.refs_4_
  14.0 2.9 %collective-permute-done.2.refs_5_ = bf16[128,256]{1,0:T(8,128)(2,1)S(1)} collective-permute-done((bf16[128,256]{1,0:T(8,128)(2,1)}, bf16[128,256]{1,0:T(8,128)(2,1)S(1)}, u32[]{:S(2)}, u32[]{:S(2)}) %collective-permute-start.2) | collective-permute-done | bytes 65568 | tf_op jit(solution)/shard_map/ppermute | solution.py:255
  16.9 1.2 %collective-permute-done.3.refs_6_ = bf16[128,256]{1,0:T(8,128)(2,1)S(1)} collective-permute-done((bf16[128,256]{1,0:T(8,128)(2,1)}, bf16[128,256]{1,0:T(8,128)(2,1)S(1)}, u32[]{:S(2)}, u32[]{:S(2)}) %collective-permute-start.3) | collective-permute-done | bytes 65568 | tf_op jit(solution)/shard_map/ppermute | solution.py:255
  18.1 1.2 %collective-permute-done.4.refs_7_ = bf16[128,256]{1,0:T(8,128)(2,1)S(1)} collective-permute-done((bf16[128,256]{1,0:T(8,128)(2,1)}, bf16[128,256]{1,0:T(8,128)(2,1)S(1)}, u32[]{:S(2)}, u32[]{:S(2)}) %collective-permute-start.4) | collective-permute-done | bytes 65568 | tf_op jit(solution)/shard_map/ppermute | solution.py:255
  19.3 0.0 copy-done
  19.3 0.0 copy-done.3
  19.3 0.0 copy-done.4
  19.3 0.0 copy-done.1
  19.3 0.0 copy-done.2
  19.3 0.0 copy-done.6
  19.3 0.0 copy-start.5
  19.3 0.8 %copy-done.5 = bf16[128,256]{1,0:T(8,128)(2,1)S(1)} copy-done((bf16[128,256]{1,0:T(8,128)(2,1)S(1)}, bf16[128,256]{1,0:T(8,128)(2,1)}, u32[]{:S(2)}) %copy-start.5) | copy-done | bytes 65560
  20.2 9.5 %degrid.1 = bf16[256,128]{1,0:T(8,128)(2,1)S(1)} custom-call(s32[32]{0:T(128)S(1)} %copy-done.6, f32[256,8]{1,0:T(8,128)S(1)} %copy.12.refs_1_, bf16[512,256]{1,0:T(8,128)(2,1)S(1)} %copy-done, bf16[128,256]{1,0:T(8,128)(2,1)S(1)} %copy-done.5, bf16[128,256]{1,0:T(8,128)(2,1)S(1)} %collective-permute-done.1.refs_4_, ...), custom_call_target="tpu_custom_call" | custom-call | tf_op jit(solution)/shard_map/degrid/pallas_call | solution.py:257
  29.7 11.1 %all_to_all.5 = bf16[16,16,128]{2,1,0:T(8,128)(2,1)} all-to-all(bf16[16,16,128]{2,1,0:T(8,128)(2,1)S(1)} %bitcast.3), channel_id=1, replica_groups=mesh['grp'=2,'row'=16] {'row'}, dimensions={0} | all-to-all | bytes 131072 | tf_op jit(solution)/shard_map/all_to_all | solution.py:279
  40.7 1.5 %place.1 = f32[2,32,512]{2,1,0:T(8,128)} custom-call(bf16[256,128]{1,0:T(8,128)(2,1)} %bitcast.4), custom_call_target="tpu_custom_call" | custom-call | tf_op jit(solution)/shard_map/place/pallas_call | solution.py:282
  (1 shorter events, 0.0 us)
Async XLA Ops:
  0.0 1.8 %collective-permute-start = (bf16[2,16,32,128]{3,2,1,0:T(8,128)(2,1)}, bf16[2,16,32,128]{3,2,1,0:T(8,128)(2,1)S(1)}, u32[]{:S(2)}, u32[]{:S(2)}) collective-permute-start(bf16[2,16,32,128]{3,2,1,0:T(8,128)(2,1)} %refs_4_.1), channel_id=1, source_target_pairs={{0,1},{1,0},{2,3},{3,2},{4,5},{5,4},{6,7},{7,6},{8,9},{9,8},{10,11... | collective-permute-start | bytes 786440 | tf_op jit(solution)/shard_map/ppermute | solution.py:238
  1.8 0.7 %copy-start.7 = (bf16[2,16,32,128]{3,2,1,0:T(8,128)(2,1)}, bf16[2,16,32,128]{3,2,1,0:T(8,128)(2,1)S(1)}, u32[]{:S(2)}) copy-start(bf16[2,16,32,128]{3,2,1,0:T(8,128)(2,1)S(1)} %collective-permute-done.refs_5_) | copy-start | bytes 786436
  2.5 11.3 %copy-start.8 = (f32[256,8]{0,1:T(8,128)S(1)}, f32[256,8]{0,1:T(8,128)}, u32[]{:S(2)}) copy-start(f32[256,8]{0,1:T(8,128)} %param.16) | copy-start | bytes 24580
  2.5 16.8 %copy-start = (bf16[512,256]{1,0:T(8,128)(2,1)S(1)}, bf16[512,256]{1,0:T(8,128)(2,1)}, u32[]{:S(2)}) copy-start(bf16[512,256]{1,0:T(8,128)(2,1)} %constant.2.clone.refs_2_) | copy-start | bytes 786436
  2.5 16.8 %copy-start.3 = (s32[2,8192]{1,0:T(2,128)S(1)}, s32[2,8192]{1,0:T(2,128)}, u32[]{:S(2)}) copy-start(s32[2,8192]{1,0:T(2,128)} %refs_10_.1) | copy-start | bytes 196612
  2.5 16.8 %copy-start.4 = (s32[2,8192]{1,0:T(2,128)S(1)}, s32[2,8192]{1,0:T(2,128)}, u32[]{:S(2)}) copy-start(s32[2,8192]{1,0:T(2,128)} %refs_11_.1) | copy-start | bytes 196612
  6.5 7.5 %collective-permute-start.1 = (bf16[128,256]{1,0:T(8,128)(2,1)}, bf16[128,256]{1,0:T(8,128)(2,1)S(1)}, u32[]{:S(2)}, u32[]{:S(2)}) collective-permute-start(bf16[128,256]{1,0:T(8,128)(2,1)} %get-tuple-element.11), channel_id=1, source_target_pairs={{0,2},{1,3},{2,0},{3,1},{4,6},{5,7},{6,4},{7,5},{8,10},{9,11},{10,... | collective-permute-start | bytes 196616 | tf_op jit(solution)/shard_map/ppermute | solution.py:255
  9.4 7.5 %collective-permute-start.2 = (bf16[128,256]{1,0:T(8,128)(2,1)}, bf16[128,256]{1,0:T(8,128)(2,1)S(1)}, u32[]{:S(2)}, u32[]{:S(2)}) collective-permute-start(bf16[128,256]{1,0:T(8,128)(2,1)} %get-tuple-element.12), channel_id=1, source_target_pairs={{0,14},{1,15},{2,4},{3,5},{4,2},{5,3},{6,8},{7,9},{8,6},{9,7},{10,... | collective-permute-start | bytes 196616 | tf_op jit(solution)/shard_map/ppermute | solution.py:255
  12.9 5.2 %collective-permute-start.3 = (bf16[128,256]{1,0:T(8,128)(2,1)}, bf16[128,256]{1,0:T(8,128)(2,1)S(1)}, u32[]{:S(2)}, u32[]{:S(2)}) collective-permute-start(bf16[128,256]{1,0:T(8,128)(2,1)} %get-tuple-element.13), channel_id=1, source_target_pairs={{0,4},{1,5},{2,6},{3,7},{4,0},{5,1},{6,2},{7,3},{8,12},{9,13},{10,... | collective-permute-start | bytes 196616 | tf_op jit(solution)/shard_map/ppermute | solution.py:255
  12.9 6.4 %copy-start.1 = (s32[2,8192]{1,0:T(2,128)S(1)}, s32[2,8192]{1,0:T(2,128)}, u32[]{:S(2)}) copy-start(s32[2,8192]{1,0:T(2,128)} %refs_8_.1) | copy-start | bytes 196612
  12.9 6.4 %copy-start.2 = (s32[2,8192]{1,0:T(2,128)S(1)}, s32[2,8192]{1,0:T(2,128)}, u32[]{:S(2)}) copy-start(s32[2,8192]{1,0:T(2,128)} %refs_9_.1) | copy-start | bytes 196612
  12.9 6.4 %collective-permute-start.4 = (bf16[128,256]{1,0:T(8,128)(2,1)}, bf16[128,256]{1,0:T(8,128)(2,1)S(1)}, u32[]{:S(2)}, u32[]{:S(2)}) collective-permute-start(bf16[128,256]{1,0:T(8,128)(2,1)} %get-tuple-element.14), channel_id=1, source_target_pairs={{0,12},{1,13},{2,14},{3,15},{4,8},{5,9},{6,10},{7,11},{8,4},{9,5},... | collective-permute-start | bytes 196616 | tf_op jit(solution)/shard_map/ppermute | solution.py:255
  13.9 5.4 %copy-start.6 = (s32[32]{0:T(128)S(1)}, s32[32]{0:T(128)}, u32[]{:S(2)}) copy-start(s32[32]{0:T(128)} %refs_0_.3) | copy-start | bytes 388
  19.3 0.8 %copy-start.5 = (bf16[128,256]{1,0:T(8,128)(2,1)S(1)}, bf16[128,256]{1,0:T(8,128)(2,1)}, u32[]{:S(2)}) copy-start(bf16[128,256]{1,0:T(8,128)(2,1)} %get-tuple-element.10.refs_3_) | copy-start | bytes 196612
where the time goes:
time: 42.5 us; the launch traced here: 42.3 us
  Pallas kernels  14.9 us (35%)
  blocking collectives  11.1 us (26%)
  starting transfers between devices  7.78 us (18%)
  waiting for transfers between devices  6.71 us (16%)
  local copies, waits for them, and re-layouts  1.69 us (4%)
    all_to_all x1, blocking collectives, local(): lax.all_to_all(results.reshape(devices, 4 * chunks, LANES), 'row', split_...  11.1 us
    pallas_call x1, Pallas kernels, local(): pl.pallas_call(lambda *refs: degrid_kernel(devices, per_dest, *refs), out...  9.49 us
    ppermute x4, starting transfers between devices, local(): came.append(lax.ppermute(pieces[1 + pairing], 'row', pairs))  7.33 us
    ppermute x4, waiting for transfers between devices, local(): came.append(lax.ppermute(pieces[1 + pairing], 'row', pairs))  5.33 us
    pallas_call x1, Pallas kernels, local(): pl.pallas_call(lambda *refs: facet_kernel(devices, *refs), out_shape=[pie...  3.93 us
    unnamed x19, local copies, waits for them, and re-layouts  1.69 us
    pallas_call x1, Pallas kernels, local(): pl.pallas_call(lambda *refs: place_kernel(devices, chunks, *refs), out_sh...  1.53 us
    ppermute x1, waiting for transfers between devices, local(): lax.ppermute(facet_rows, 'row', [(i, i ^ 1) for i in range(devices)])  1.37 us
  transfers between devices with their start and end apart: 5, of which 4 were waited for; matrix products, arithmetic and copies ran while one was open for 0% of the time, Pallas kernels for 0%

commit v1 on v0

--- a/solution.py
+++ b/solution.py
@@ -17,6 +17,8 @@
 NOVER = 256
 CHIP = 2 * R_DEV
 LANES = 128
+BLOCK = 1024
+UNROLL = 4
 
 TWO_PI = 2.0 * math.pi
 
@@ -36,71 +38,66 @@
     return np.ascontiguousarray(np.concatenate([upper, lower], axis=0).T)
 
 
-def partners(chip, chips):
-    return [
-        chip ^ 1,
-        (((chip + 1) ^ 1) + chips - 1) % chips,
-        chip ^ 2,
-        (((chip + 2) ^ 2) + chips - 2) % chips,
-    ]
-
-
-def facet_kernel(
-    devices,
-    start_ref,
-    length_ref,
-    offset_ref,
-    window_ref,
-    own_ref,
-    other_ref,
-    *rest,
-):
-    outs, padded = rest[:5], rest[5]
+SHIFTS = (1, 2, -2, -1)
+
+
+def facet_kernel(devices, start_ref, length_ref, offset_ref, window_ref, rows_ref, *rest, other):
+    if other:
+        earlier, outs, padded = rest[:5], rest[5:10], rest[10]
+    else:
+        earlier, outs, padded = None, rest[:5], rest[5]
     total_rows = devices * R_DEV
     chips = devices // 2
     position = lax.axis_index("row")
     chip = position // 2
     core = position % 2
+    half = 1 - core if other else core
+    base = chip * CHIP + half * R_DEV
     padded[:R_DEV, :] = jnp.zeros((R_DEV, F), jnp.float32)
     padded[R_DEV + SUB :, :] = jnp.zeros((R_DEV, F), jnp.float32)
     padded[R_DEV : R_DEV + SUB, :] = jnp.transpose(window_ref[...])
-    targets = [chip] + partners(chip, chips)
     row_index = lax.broadcasted_iota(jnp.int32, (R_DEV, F), 0)
-    for held, source in enumerate((own_ref, other_ref)):
-        half = core if held == 0 else 1 - core
-        base = chip * CHIP + half * R_DEV
-        turns = (offset_ref[...] * (base + row_index)) & (total_rows - 1)
-        angles = TWO_PI * turns.astype(jnp.float32) / total_rows
-        cosines = jnp.cos(angles)
-        sines = jnp.sin(angles)
-        weights = []
-        for target in targets:
+    turns = (offset_ref[...] * (base + row_index)) & (total_rows - 1)
+    angles = TWO_PI * turns.astype(jnp.float32) / total_rows
+    cosines = jnp.cos(angles)
+    sines = jnp.sin(angles)
+    weights = []
+    for shift in (0,) + SHIFTS:
+        target = (chip + chips + shift) % chips
+        for sub in range(SUB_DEV):
+            subgrid = (target * 2 + core) * SUB_DEV + sub
+            slot = (base - start_ref[subgrid]) & (total_rows - 1)
+            slot = jnp.where(slot > total_rows - R_DEV, slot - total_rows, slot)
+            slot = jnp.minimum(slot, SUB)
+            piece = padded[pl.ds(slot + R_DEV, R_DEV), :]
+            weights.append(jnp.where(slot + row_index < length_ref[subgrid], piece, 0.0))
+    for tile in range(R_DEV // 16):
+        rows = slice(16 * tile, 16 * tile + 16)
+        sums = [[None, None] for _ in weights]
+        for f in range(F):
+            real_in = rows_ref[0, f, rows, :].astype(jnp.float32)
+            imag_in = rows_ref[1, f, rows, :].astype(jnp.float32)
+            cos_f = cosines[rows, f : f + 1]
+            sin_f = sines[rows, f : f + 1]
+            real_part = cos_f * real_in - sin_f * imag_in
+            imag_part = cos_f * imag_in + sin_f * real_in
+            for entry, weight in zip(sums, weights):
+                w = jnp.broadcast_to(weight[rows, f : f + 1], (16, KC))
+                entry[0] = w * real_part if f == 0 else entry[0] + w * real_part
+                entry[1] = w * imag_part if f == 0 else entry[1] + w * imag_part
+        for place, entry in enumerate(sums):
+            out, sub = outs[place // SUB_DEV], place % SUB_DEV
+            if other:
+                first = pl.multiple_of(sub * CHIP + half * R_DEV + 16 * tile, 16)
+            else:
+                first = sub * R_DEV + 16 * tile
+            out[pl.ds(first, 16), :KC] = entry[0].astype(jnp.bfloat16)
+            out[pl.ds(first, 16), KC:] = entry[1].astype(jnp.bfloat16)
+    if other:
+        for piece, out in zip(earlier, outs):
             for sub in range(SUB_DEV):
-                subgrid = (target * 2 + core) * SUB_DEV + sub
-                slot = (base - start_ref[subgrid]) & (total_rows - 1)
-                slot = jnp.where(slot > total_rows - R_DEV, slot - total_rows, slot)
-                slot = jnp.minimum(slot, SUB)
-                piece = padded[pl.ds(slot + R_DEV, R_DEV), :]
-                weights.append(jnp.where(slot + row_index < length_ref[subgrid], piece, 0.0))
-        for tile in range(R_DEV // 16):
-            rows = slice(16 * tile, 16 * tile + 16)
-            sums = [[None, None] for _ in weights]
-            for f in range(F):
-                real_in = source[0, f, rows, :].astype(jnp.float32)
-                imag_in = source[1, f, rows, :].astype(jnp.float32)
-                cos_f = cosines[rows, f : f + 1]
-                sin_f = sines[rows, f : f + 1]
-                real_part = cos_f * real_in - sin_f * imag_in
-                imag_part = cos_f * imag_in + sin_f * real_in
-                for entry, weight in zip(sums, weights):
-                    w = jnp.broadcast_to(weight[rows, f : f + 1], (16, KC))
-                    entry[0] = w * real_part if f == 0 else entry[0] + w * real_part
-                    entry[1] = w * imag_part if f == 0 else entry[1] + w * imag_part
-            for place, entry in enumerate(sums):
-                first = pl.multiple_of((place % SUB_DEV) * CHIP + half * R_DEV + 16 * tile, 16)
-                out = outs[place // SUB_DEV]
-                out[pl.ds(first, 16), :KC] = entry[0].astype(jnp.bfloat16)
-                out[pl.ds(first, 16), KC:] = entry[1].astype(jnp.bfloat16)
+                first = pl.multiple_of(sub * CHIP + core * R_DEV, R_DEV)
+                out[pl.ds(first, R_DEV), :] = piece[sub * R_DEV : (sub + 1) * R_DEV, :]
 
 
 def taps(low, high, cell, table_row):
@@ -130,10 +127,10 @@
     table_ref,
     transform_ref,
     own_ref,
-    first_ref,
-    second_ref,
-    third_ref,
-    fourth_ref,
+    below_ref,
+    far_below_ref,
+    far_above_ref,
+    above_ref,
     row_ref,
     column_ref,
     row_kernel_ref,
@@ -144,20 +141,18 @@
 ):
     position = lax.axis_index("row")
     chip = position // 2
-    even = chip % 2 == 0
-    table = jnp.transpose(table_ref[...])
+    table = table_ref[...]
     near = table.astype(jnp.bfloat16).astype(jnp.float32)
     near_low, near_high = near[:, :LANES], near[:, LANES:]
     table_low, table_high = table[:, :LANES], table[:, LANES:]
     for sub in range(SUB_DEV):
         rows = slice(sub * CHIP, sub * CHIP + CHIP)
-        first, second = first_ref[rows, :], second_ref[rows, :]
         summed = jnp.concatenate(
             [
                 own_ref[rows, :],
-                jnp.where(even, first, second),
-                third_ref[rows, :] + fourth_ref[rows, :],
-                jnp.where(even, second, first),
+                above_ref[rows, :],
+                far_below_ref[rows, :] + far_above_ref[rows, :],
+                below_ref[rows, :],
             ],
             axis=0,
         )
@@ -165,8 +160,10 @@
             transform_ref[...], summed, (((1,), (1,)), ((), ())), preferred_element_type=jnp.float32
         ).astype(jnp.bfloat16)
 
-    def one_dest(dest, carry):
-        lanes = pl.ds(pl.multiple_of(dest * per_dest, per_dest), per_dest)
+    chunks = per_dest // LANES
+
+    def one_block(block, carry):
+        lanes = pl.ds(pl.multiple_of(block * BLOCK, BLOCK), BLOCK)
         for sub in range(SUB_DEV):
             subgrid = position * SUB_DEV + sub
             shift = start_ref[subgrid] - chip * CHIP
@@ -197,15 +194,14 @@
                 jnp.sum(weights * real_part, axis=0, keepdims=True),
                 jnp.sum(weights * imag_part, axis=0, keepdims=True),
             ]
-            chunks = per_dest // LANES
+            first = block * (BLOCK // LANES * 4)
             for part in range(2):
-                for chunk in range(chunks):
-                    gathered[pl.ds(dest * 4 * chunks + (sub * 2 + part) * chunks + chunk, 1), :] = sums[part][
-                        :, chunk * LANES : (chunk + 1) * LANES
-                    ]
+                for place in range(BLOCK // LANES):
+                    row = place // chunks * 4 * chunks + (sub * 2 + part) * chunks + place % chunks
+                    gathered[pl.ds(first + row, 1), :] = sums[part][:, place * LANES : (place + 1) * LANES]
         return carry
 
-    lax.fori_loop(0, devices, one_dest, 0)
+    lax.fori_loop(0, row_ref.shape[1] // BLOCK, one_block, 0, unroll=UNROLL)
     out_ref[...] = gathered[...].astype(jnp.bfloat16)
 
 
@@ -236,23 +232,34 @@
     per_dest = slots // devices
     chunks = per_dest // LANES
     other_rows = lax.ppermute(facet_rows, "row", [(i, i ^ 1) for i in range(devices)])
-    piece = jax.ShapeDtypeStruct((SUB_DEV * CHIP, 2 * KC), jnp.bfloat16)
-    pieces = pl.pallas_call(
-        lambda *refs: facet_kernel(devices, *refs),
-        out_shape=[piece] * 5,
-        in_specs=[SMEM, SMEM, VMEM, VMEM, VMEM, VMEM],
+    small = pltpu.CompilerParams(vmem_limit_bytes=8 * 1024 * 1024)
+    tables = (range_start, range_length, facet_offset.reshape(1, F), window_table)
+    own_pieces = pl.pallas_call(
+        lambda *refs: facet_kernel(devices, *refs, other=False),
+        out_shape=[jax.ShapeDtypeStruct((SUB_DEV * R_DEV, 2 * KC), jnp.bfloat16)] * 5,
+        in_specs=[SMEM, SMEM, VMEM, VMEM, VMEM],
         out_specs=[VMEM] * 5,
         scratch_shapes=[pltpu.VMEM((SUB + 2 * R_DEV, F), jnp.float32)],
-        name="facet_sums",
-    )(range_start, range_length, facet_offset.reshape(1, F), window_table, facet_rows, other_rows)
+        compiler_params=small,
+        name="own_facet_sums",
+    )(*tables, facet_rows)
+    pieces = pl.pallas_call(
+        lambda *refs: facet_kernel(devices, *refs, other=True),
+        out_shape=[jax.ShapeDtypeStruct((SUB_DEV * CHIP, 2 * KC), jnp.bfloat16)] * 5,
+        in_specs=[SMEM, SMEM] + [VMEM] * 8,
+        out_specs=[VMEM] * 5,
+        scratch_shapes=[pltpu.VMEM((SUB + 2 * R_DEV, F), jnp.float32)],
+        compiler_params=small,
+        name="other_facet_sums",
+    )(*tables, other_rows, *own_pieces)
     came = []
-    for pairing in range(4):
+    for shift, piece in zip(SHIFTS, pieces[1:]):
         pairs = [
-            (2 * chip + core, 2 * partners(chip, chips)[pairing] + core)
+            (2 * chip + core, 2 * ((chip + shift) % chips) + core)
             for chip in range(chips)
             for core in range(2)
         ]
-        came.append(lax.ppermute(pieces[1 + pairing], "row", pairs))
+        came.append(lax.ppermute(piece, "row", pairs))
     rows_out = devices * 4 * chunks
     results = pl.pallas_call(
         lambda *refs: degrid_kernel(devices, per_dest, *refs),
@@ -267,7 +274,7 @@
         name="degrid",
     )(
         range_start,
-        kernel_table,
+        kernel_table.T,
         jnp.asarray(transform_table()),
         pieces[0],
         *came,
@@ -285,6 +292,7 @@
         in_specs=[VMEM],
         out_specs=VMEM,
         scratch_shapes=[pltpu.VMEM((rows_out, LANES), jnp.float32)],
+        compiler_params=small,
         name="place",
     )(received.reshape(rows_out, LANES))
 

time: 42.5 us -> 36.1 us (0.85)
  Pallas kernels: 14.9 us -> 10.1 us
  waiting for transfers between devices: 6.71 us -> 2.96 us
  blocking collectives: 11.1 us -> 12.1 us
  starting transfers between devices: 7.78 us -> 8.67 us
    pallas_call x1, Pallas kernels: 9.49 us -> 6.03 us  [local(): pl.pallas_call(lambda *refs: degrid_kernel(devices, per_dest, *refs), out...]
    ppermute x4, waiting for transfers between devices: 5.33 us -> 2.96 us  [local(): came.append(lax.ppermute(piece, 'row', pairs))]
    ppermute x1, waiting for transfers between devices: 1.37 us -> 0.01 us  [local(): lax.ppermute(facet_rows, 'row', [(i, i ^ 1) for i in range(devices)])]
    all_to_all x1, blocking collectives: 11.1 us -> 12.1 us  [local(): lax.all_to_all(results.reshape(devices, 4 * chunks, LANES), 'row', split_...]
    pallas_call x1, Pallas kernels: 1.53 us -> 0.69 us  [local(): pl.pallas_call(lambda *refs: place_kernel(devices, chunks, *refs), out_sh...]
    ppermute x4, starting transfers between devices: 7.33 us -> 8.15 us  [local(): came.append(lax.ppermute(piece, 'row', pairs))]
    pallas_call x1 -> x2, Pallas kernels: 3.93 us -> 3.39 us  [the longest x1 1.7 us: local(): pl.pallas_call(lambda *refs: facet_kernel(devices, *refs, other=True), ou...]
    unnamed x19 -> x22, local copies, waits for them, and re-layouts: 1.69 us -> 1.86 us
  transfers between devices with their start and end apart: 5 -> 5, of which waited for: 4 -> 3; matrix products, arithmetic and copies ran while one was open for 0% -> 0% of each run, Pallas kernels for 0% -> 5%
where the time goes in v1:
time: 36.1 us; the launch traced here: 35.8 us
  blocking collectives  12.1 us (34%)
  Pallas kernels  10.1 us (28%)
  starting transfers between devices  8.67 us (24%)
  waiting for transfers between devices  2.96 us (8%)
  local copies, waits for them, and re-layouts  1.86 us (5%)
    all_to_all x1, blocking collectives, local(): lax.all_to_all(results.reshape(devices, 4 * chunks, LANES), 'row', split_...  12.1 us
    ppermute x4, starting transfers between devices, local(): came.append(lax.ppermute(piece, 'row', pairs))  8.15 us
    pallas_call x1, Pallas kernels, local(): pl.pallas_call(lambda *refs: degrid_kernel(devices, per_dest, *refs), out...  6.03 us
    ppermute x4, waiting for transfers between devices, local(): came.append(lax.ppermute(piece, 'row', pairs))  2.96 us
    unnamed x22, local copies, waits for them, and re-layouts  1.86 us
    pallas_call x1, Pallas kernels, local(): pl.pallas_call(lambda *refs: facet_kernel(devices, *refs, other=True), ou...  1.7 us
    pallas_call x1, Pallas kernels, local(): pl.pallas_call(lambda *refs: facet_kernel(devices, *refs, other=False), o...  1.69 us
  transfers between devices with their start and end apart: 5, of which 3 were waited for; matrix products, arithmetic and copies ran while one was open for 0% of the time, Pallas kernels for 5%

profile of v1, /device:TPU:0, one launch (start us, length us, event | category | flops | bytes accessed | tf_op | source)
XLA Modules:
  0.0 35.8 jit_solution(5925186907438396615)
XLA Ops:
  0.0 0.0 copy-start.8
  0.0 0.0 copy-start.9
  0.0 0.5 %collective-permute-start = (bf16[2,16,32,128]{3,2,1,0:T(8,128)(2,1)}, bf16[2,16,32,128]{3,2,1,0:T(8,128)(2,1)S(1)}, u32[]{:S(2)}, u32[]{:S(2)}) collective-permute-start(bf16[2,16,32,128]{3,2,1,0:T(8,128)(2,1)} %refs_4_.1), channel_id=1, source_target_pairs={{0,1},{1,0},{2,3},{3,2},{4,5},{5,4},{6,7},{7,6},{8,9},{9,8},{10,11... | collective-permute-start | bytes 786440 | tf_op jit(solution)/shard_map/ppermute | solution.py:234
  0.5 0.1 copy-done.8
  0.7 0.0 copy-done.9
  0.7 0.0 copy-done.10
  0.7 0.9 %copy-done.1 = bf16[2,16,32,128]{3,2,1,0:T(8,128)(2,1)S(1)} copy-done((bf16[2,16,32,128]{3,2,1,0:T(8,128)(2,1)S(1)}, bf16[2,16,32,128]{3,2,1,0:T(8,128)(2,1)}, u32[]{:S(2)}) %copy-start.1) | copy-done | bytes 262168
  1.6 0.7 %copy-done.6 = f32[16,256]{1,0:T(8,128)S(1)} copy-done((f32[16,256]{1,0:T(8,128)S(1)}, f32[16,256]{1,0:T(8,128)}, u32[]{:S(2)}) %copy-start.6) | copy-done | bytes 16408
  2.4 1.7 %own_facet_sums.1 = (bf16[64,256]{1,0:T(8,128)(2,1)S(1)}, bf16[64,256]{1,0:T(8,128)(2,1)S(1)}, bf16[64,256]{1,0:T(8,128)(2,1)S(1)}, bf16[64,256]{1,0:T(8,128)(2,1)S(1)}, bf16[64,256]{1,0:T(8,128)(2,1)S(1)}) custom-call(s32[32]{0:T(128)S(1)} %copy-done.8, s32[32]{0:T(128)S(1)} %copy-done.9, s32[1,16]{1,0:T(1,128)S(1)} %bitcast.7, f32[16,256]{1,0:T(8,128)S(1)} %copy-done.6, ...), custom_call_target="tpu_custom_call" | custom-call | tf_op jit(solution)/shard_map/own_facet_sums/pallas_call | solution.py:237
  4.1 0.0 copy-start
  4.1 0.0 collective-permute-done.refs_4_
  4.1 0.0 copy-start.2
  4.1 0.0 copy-start.3
  4.1 0.0 copy-start.4
  4.1 1.7 %other_facet_sums.1 = (bf16[128,256]{1,0:T(8,128)(2,1)S(1)}, bf16[128,256]{1,0:T(8,128)(2,1)S(1)}, bf16[128,256]{1,0:T(8,128)(2,1)S(1)}, bf16[128,256]{1,0:T(8,128)(2,1)S(1)}, bf16[128,256]{1,0:T(8,128)(2,1)S(1)}) custom-call(s32[32]{0:T(128)S(1)} %copy-done.8, s32[32]{0:T(128)S(1)} %copy-done.9, s32[1,16]{1,0:T(1,128)S(1)} %bitcast.8, ...), custom_call_target="tpu_custom_call" | custom-call | tf_op jit(solution)/shard_map/other_facet_sums/pallas_call | solution.py:246
  5.8 3.0 %collective-permute-start.1 = (bf16[128,256]{1,0:T(8,128)(2,1)S(1)}, bf16[128,256]{1,0:T(8,128)(2,1)S(1)}, u32[]{:S(2)}, u32[]{:S(2)}) collective-permute-start(bf16[128,256]{1,0:T(8,128)(2,1)S(1)} %get-tuple-element.21), channel_id=1, source_target_pairs={{0,2},{1,3},{2,4},{3,5},{4,6},{5,7},{6,8},{7,9},{8,10},{9,11},{10,... | collective-permute-start | bytes 196616 | tf_op jit(solution)/shard_map/ppermute | solution.py:262
  8.8 1.6 %collective-permute-start.2 = (bf16[128,256]{1,0:T(8,128)(2,1)S(1)}, bf16[128,256]{1,0:T(8,128)(2,1)S(1)}, u32[]{:S(2)}, u32[]{:S(2)}) collective-permute-start(bf16[128,256]{1,0:T(8,128)(2,1)S(1)} %get-tuple-element.22), channel_id=1, source_target_pairs={{0,4},{1,5},{2,6},{3,7},{4,8},{5,9},{6,10},{7,11},{8,12},{9,13},{1... | collective-permute-start | bytes 196616 | tf_op jit(solution)/shard_map/ppermute | solution.py:262
  10.4 2.2 %collective-permute-start.3 = (bf16[128,256]{1,0:T(8,128)(2,1)S(1)}, bf16[128,256]{1,0:T(8,128)(2,1)S(1)}, u32[]{:S(2)}, u32[]{:S(2)}) collective-permute-start(bf16[128,256]{1,0:T(8,128)(2,1)S(1)} %get-tuple-element.23), channel_id=1, source_target_pairs={{0,12},{1,13},{2,14},{3,15},{4,0},{5,1},{6,2},{7,3},{8,4},{9,5},{1... | collective-permute-start | bytes 196616 | tf_op jit(solution)/shard_map/ppermute | solution.py:262
  12.7 1.3 %collective-permute-start.4 = (bf16[128,256]{1,0:T(8,128)(2,1)S(1)}, bf16[128,256]{1,0:T(8,128)(2,1)S(1)}, u32[]{:S(2)}, u32[]{:S(2)}) collective-permute-start(bf16[128,256]{1,0:T(8,128)(2,1)S(1)} %get-tuple-element.24), channel_id=1, source_target_pairs={{0,14},{1,15},{2,0},{3,1},{4,2},{5,3},{6,4},{7,5},{8,6},{9,7},{10,... | collective-permute-start | bytes 196616 | tf_op jit(solution)/shard_map/ppermute | solution.py:262
  14.0 0.6 %collective-permute-done.1.refs_4_ = bf16[128,256]{1,0:T(8,128)(2,1)S(1)} collective-permute-done((bf16[128,256]{1,0:T(8,128)(2,1)S(1)}, bf16[128,256]{1,0:T(8,128)(2,1)S(1)}, u32[]{:S(2)}, u32[]{:S(2)}) %collective-permute-start.1) | collective-permute-done | bytes 65568 | tf_op jit(solution)/shard_map/ppermute | solution.py:262
  14.6 0.8 %collective-permute-done.2.refs_5_ = bf16[128,256]{1,0:T(8,128)(2,1)S(1)} collective-permute-done((bf16[128,256]{1,0:T(8,128)(2,1)S(1)}, bf16[128,256]{1,0:T(8,128)(2,1)S(1)}, u32[]{:S(2)}, u32[]{:S(2)}) %collective-permute-start.2) | collective-permute-done | bytes 65568 | tf_op jit(solution)/shard_map/ppermute | solution.py:262
  15.4 0.0 collective-permute-done.3.refs_6_
  15.4 1.5 %collective-permute-done.4.refs_7_ = bf16[128,256]{1,0:T(8,128)(2,1)S(1)} collective-permute-done((bf16[128,256]{1,0:T(8,128)(2,1)S(1)}, bf16[128,256]{1,0:T(8,128)(2,1)S(1)}, u32[]{:S(2)}, u32[]{:S(2)}) %collective-permute-start.4) | collective-permute-done | bytes 65568 | tf_op jit(solution)/shard_map/ppermute | solution.py:262
  16.9 0.0 copy-done.5
  16.9 0.0 copy-done.7
  16.9 0.0 copy-done
  16.9 0.0 copy-done.2
  16.9 0.0 copy-done.3
  17.0 0.0 copy-done.4
  17.0 6.0 %degrid.1 = bf16[256,128]{1,0:T(8,128)(2,1)S(1)} custom-call(s32[32]{0:T(128)S(1)} %copy-done.8, f32[8,256]{1,0:T(8,128)S(1)} %bitcast.6, bf16[512,256]{1,0:T(8,128)(2,1)S(1)} %copy-done, bf16[128,256]{1,0:T(8,128)(2,1)S(1)} %get-tuple-element.20.refs_3_, bf16[128,256]{1,0:T(8,128)(2,1)S(1)} %collective-permute-done.1.refs_4_, ...), custom_call_target="tpu_custom_call" | custom-call | tf_op jit(solution)/shard_map/degrid/pallas_call | solution.py:264
  23.0 12.1 %all_to_all.5 = bf16[16,16,128]{2,1,0:T(8,128)(2,1)S(1)} all-to-all(bf16[16,16,128]{2,1,0:T(8,128)(2,1)S(1)} %bitcast.4), channel_id=1, replica_groups=mesh['grp'=2,'row'=16] {'row'}, dimensions={0} | all-to-all | bytes 131072 | tf_op jit(solution)/shard_map/all_to_all | solution.py:286
  35.1 0.7 %place.1 = f32[2,32,512]{2,1,0:T(8,128)} custom-call(bf16[256,128]{1,0:T(8,128)(2,1)S(1)} %bitcast.5), custom_call_target="tpu_custom_call" | custom-call | tf_op jit(solution)/shard_map/place/pallas_call | solution.py:289
  (5 shorter events, 0.0 us)
Async XLA Ops:
  0.0 0.7 %copy-start.8 = (s32[32]{0:T(128)S(1)}, s32[32]{0:T(128)}, u32[]{:S(2)}) copy-start(s32[32]{0:T(128)} %refs_0_.5) | copy-start | bytes 388
  0.0 0.7 %copy-start.9 = (s32[32]{0:T(128)S(1)}, s32[32]{0:T(128)}, u32[]{:S(2)}) copy-start(s32[32]{0:T(128)} %refs_1_.3) | copy-start | bytes 388
  0.0 0.7 %copy-start.10 = (s32[16]{0:T(128)S(1)}, s32[16]{0:T(128)}, u32[]{:S(2)}) copy-start(s32[16]{0:T(128)} %param.14) | copy-start | bytes 196
  0.0 4.1 %collective-permute-start = (bf16[2,16,32,128]{3,2,1,0:T(8,128)(2,1)}, bf16[2,16,32,128]{3,2,1,0:T(8,128)(2,1)S(1)}, u32[]{:S(2)}, u32[]{:S(2)}) collective-permute-start(bf16[2,16,32,128]{3,2,1,0:T(8,128)(2,1)} %refs_4_.1), channel_id=1, source_target_pairs={{0,1},{1,0},{2,3},{3,2},{4,5},{5,4},{6,7},{7,6},{8,9},{9,8},{10,11... | collective-permute-start | bytes 786440 | tf_op jit(solution)/shard_map/ppermute | solution.py:234
  0.7 0.9 %copy-start.1 = (bf16[2,16,32,128]{3,2,1,0:T(8,128)(2,1)S(1)}, bf16[2,16,32,128]{3,2,1,0:T(8,128)(2,1)}, u32[]{:S(2)}) copy-start(bf16[2,16,32,128]{3,2,1,0:T(8,128)(2,1)} %refs_4_.1) | copy-start | bytes 786436
  1.6 0.7 %copy-start.6 = (f32[16,256]{1,0:T(8,128)S(1)}, f32[16,256]{1,0:T(8,128)}, u32[]{:S(2)}) copy-start(f32[16,256]{1,0:T(8,128)} %refs_3_.3) | copy-start | bytes 49156
  2.4 14.6 %copy-start.5 = (s32[2,8192]{1,0:T(2,128)S(1)}, s32[2,8192]{1,0:T(2,128)}, u32[]{:S(2)}) copy-start(s32[2,8192]{1,0:T(2,128)} %refs_11_.1) | copy-start | bytes 196612
  2.4 14.6 %copy-start.7 = (f32[256,8]{0,1:T(8,128)S(1)}, f32[256,8]{0,1:T(8,128)}, u32[]{:S(2)}) copy-start(f32[256,8]{0,1:T(8,128)} %param.16) | copy-start | bytes 24580
  4.1 12.9 %copy-start = (bf16[512,256]{1,0:T(8,128)(2,1)S(1)}, bf16[512,256]{1,0:T(8,128)(2,1)}, u32[]{:S(2)}) copy-start(bf16[512,256]{1,0:T(8,128)(2,1)} %constant.2.clone.refs_2_) | copy-start | bytes 786436
  4.1 12.9 %copy-start.2 = (s32[2,8192]{1,0:T(2,128)S(1)}, s32[2,8192]{1,0:T(2,128)}, u32[]{:S(2)}) copy-start(s32[2,8192]{1,0:T(2,128)} %refs_8_.1) | copy-start | bytes 196612
  4.1 12.9 %copy-start.3 = (s32[2,8192]{1,0:T(2,128)S(1)}, s32[2,8192]{1,0:T(2,128)}, u32[]{:S(2)}) copy-start(s32[2,8192]{1,0:T(2,128)} %refs_9_.1) | copy-start | bytes 196612
  4.1 12.9 %copy-start.4 = (s32[2,8192]{1,0:T(2,128)S(1)}, s32[2,8192]{1,0:T(2,128)}, u32[]{:S(2)}) copy-start(s32[2,8192]{1,0:T(2,128)} %refs_10_.1) | copy-start | bytes 196612
  5.8 8.8 %collective-permute-start.1 = (bf16[128,256]{1,0:T(8,128)(2,1)S(1)}, bf16[128,256]{1,0:T(8,128)(2,1)S(1)}, u32[]{:S(2)}, u32[]{:S(2)}) collective-permute-start(bf16[128,256]{1,0:T(8,128)(2,1)S(1)} %get-tuple-element.21), channel_id=1, source_target_pairs={{0,2},{1,3},{2,4},{3,5},{4,6},{5,7},{6,8},{7,9},{8,10},{9,11},{10,... | collective-permute-start | bytes 196616 | tf_op jit(solution)/shard_map/ppermute | solution.py:262
  8.8 6.6 %collective-permute-start.2 = (bf16[128,256]{1,0:T(8,128)(2,1)S(1)}, bf16[128,256]{1,0:T(8,128)(2,1)S(1)}, u32[]{:S(2)}, u32[]{:S(2)}) collective-permute-start(bf16[128,256]{1,0:T(8,128)(2,1)S(1)} %get-tuple-element.22), channel_id=1, source_target_pairs={{0,4},{1,5},{2,6},{3,7},{4,8},{5,9},{6,10},{7,11},{8,12},{9,13},{1... | collective-permute-start | bytes 196616 | tf_op jit(solution)/shard_map/ppermute | solution.py:262
  10.4 5.0 %collective-permute-start.3 = (bf16[128,256]{1,0:T(8,128)(2,1)S(1)}, bf16[128,256]{1,0:T(8,128)(2,1)S(1)}, u32[]{:S(2)}, u32[]{:S(2)}) collective-permute-start(bf16[128,256]{1,0:T(8,128)(2,1)S(1)} %get-tuple-element.23), channel_id=1, source_target_pairs={{0,12},{1,13},{2,14},{3,15},{4,0},{5,1},{6,2},{7,3},{8,4},{9,5},{1... | collective-permute-start | bytes 196616 | tf_op jit(solution)/shard_map/ppermute | solution.py:262
  12.7 4.3 %collective-permute-start.4 = (bf16[128,256]{1,0:T(8,128)(2,1)S(1)}, bf16[128,256]{1,0:T(8,128)(2,1)S(1)}, u32[]{:S(2)}, u32[]{:S(2)}) collective-permute-start(bf16[128,256]{1,0:T(8,128)(2,1)S(1)} %get-tuple-element.24), channel_id=1, source_target_pairs={{0,14},{1,15},{2,0},{3,1},{4,2},{5,3},{6,4},{7,5},{8,6},{9,7},{10,... | collective-permute-start | bytes 196616 | tf_op jit(solution)/shard_map/ppermute | solution.py:262

commit v2 on v1

--- a/solution.py
+++ b/solution.py
@@ -23,7 +23,7 @@
 TWO_PI = 2.0 * math.pi
 
 VMEM = pl.BlockSpec(memory_space=pltpu.VMEM)
-SMEM = pl.BlockSpec(memory_space=pltpu.SMEM)
+HBM = pl.BlockSpec(memory_space=pltpu.HBM)
 
 
 def transform_table():
@@ -41,63 +41,129 @@
 SHIFTS = (1, 2, -2, -1)
 
 
-def facet_kernel(devices, start_ref, length_ref, offset_ref, window_ref, rows_ref, *rest, other):
-    if other:
-        earlier, outs, padded = rest[:5], rest[5:10], rest[10]
-    else:
-        earlier, outs, padded = None, rest[:5], rest[5]
+def facet_products(factors, rows_ref, outs, half_step, first_row):
+    for group in range(R_DEV // 16):
+        rows = slice(16 * group, 16 * group + 16)
+        cells = jnp.concatenate(
+            [rows_ref[0, :, rows, :].reshape(F * 16, KC), rows_ref[1, :, rows, :].reshape(F * 16, KC)], axis=1
+        )
+        products = []
+        for kind in range(2):
+            high = jnp.dot(factors(group, 2 * kind), cells, preferred_element_type=jnp.float32)
+            low = jnp.dot(factors(group, 2 * kind + 1), cells, preferred_element_type=jnp.float32)
+            products.append(high + low)
+        with_cos, with_sin = products
+        real_part = (with_cos[:, :KC] - with_sin[:, KC:]).astype(jnp.bfloat16)
+        imag_part = (with_cos[:, KC:] + with_sin[:, :KC]).astype(jnp.bfloat16)
+        for place, out in enumerate(outs):
+            for sub in range(SUB_DEV):
+                here = slice((place * SUB_DEV + sub) * 16, (place * SUB_DEV + sub) * 16 + 16)
+                first = first_row + sub * half_step + 16 * group
+                if not isinstance(first, int):
+                    first = pl.multiple_of(first, 16)
+                out[pl.ds(first, 16), :KC] = real_part[here]
+                out[pl.ds(first, 16), KC:] = imag_part[here]
+
+
+def own_facet_kernel(
+    devices,
+    start_hbm,
+    length_hbm,
+    offset_hbm,
+    window_hbm,
+    rows_hbm,
+    *rest,
+):
+    outs, other_factors, shifts = rest[:5], rest[5], rest[6]
+    start, length, offset, window, rows_ref, own_factors, padded, sems = rest[7:]
+    copies = [
+        pltpu.make_async_copy(source, target, sems.at[number])
+        for number, (source, target) in enumerate(
+            (
+                (start_hbm, start),
+                (length_hbm, length),
+                (offset_hbm, offset),
+                (window_hbm, window),
+                (rows_hbm, rows_ref),
+            )
+        )
+    ]
+    for copy in copies:
+        copy.start()
     total_rows = devices * R_DEV
     chips = devices // 2
     position = lax.axis_index("row")
     chip = position // 2
     core = position % 2
-    half = 1 - core if other else core
-    base = chip * CHIP + half * R_DEV
     padded[:R_DEV, :] = jnp.zeros((R_DEV, F), jnp.float32)
     padded[R_DEV + SUB :, :] = jnp.zeros((R_DEV, F), jnp.float32)
-    padded[R_DEV : R_DEV + SUB, :] = jnp.transpose(window_ref[...])
     row_index = lax.broadcasted_iota(jnp.int32, (R_DEV, F), 0)
-    turns = (offset_ref[...] * (base + row_index)) & (total_rows - 1)
-    angles = TWO_PI * turns.astype(jnp.float32) / total_rows
-    cosines = jnp.cos(angles)
-    sines = jnp.sin(angles)
-    weights = []
-    for shift in (0,) + SHIFTS:
-        target = (chip + chips + shift) % chips
+    lane = lax.broadcasted_iota(jnp.int32, (R_DEV, LANES), 1)
+    sublane = lax.broadcasted_iota(jnp.int32, (R_DEV, LANES), 0)
+    diagonal = (lane & 15) == (sublane & 15)
+
+    def spread(values):
+        wide = jnp.concatenate([values, jnp.zeros((R_DEV, LANES - F), values.dtype)], axis=1)
+        return [
+            jnp.concatenate(
+                [
+                    jnp.take_along_axis(
+                        wide[row : row + 8], (lane[:8] >> 4) + 8 * side, axis=1, mode="promise_in_bounds"
+                    )
+                    for row in range(0, R_DEV, 8)
+                ],
+                axis=0,
+            )
+            for side in range(2)
+        ]
+
+    for copy in copies[:4]:
+        copy.wait()
+    padded[R_DEV : R_DEV + SUB, :] = jnp.transpose(window[...])
+    for sub in range(SUB_DEV):
+        shift = start[position * SUB_DEV + sub] - chip * CHIP
+        shifts[sub] = jnp.full((8, LANES), shift, jnp.int32)
+    for held, factors in enumerate((own_factors, other_factors)):
+        half = core if held == 0 else 1 - core
+        base = chip * CHIP + half * R_DEV
+        turns = (offset[...] * (base + row_index)) & (total_rows - 1)
+        angles = TWO_PI * turns.astype(jnp.float32) / total_rows
+        phases = [
+            [jnp.where(diagonal, side, 0.0) for side in spread(part)]
+            for part in (jnp.cos(angles), jnp.sin(angles))
+        ]
+        for place, shift in enumerate((0,) + SHIFTS):
+            target = (chip + chips + shift) % chips
+            for sub in range(SUB_DEV):
+                subgrid = (target * 2 + core) * SUB_DEV + sub
+                slot = (base - start[subgrid]) & (total_rows - 1)
+                slot = jnp.where(slot > total_rows - R_DEV, slot - total_rows, slot)
+                slot = jnp.minimum(slot, SUB)
+                piece = padded[pl.ds(slot + R_DEV, R_DEV), :]
+                weights = spread(jnp.where(slot + row_index < length[subgrid], piece, 0.0))
+                for kind in range(2):
+                    for side in range(2):
+                        exact = weights[side] * phases[kind][side]
+                        high = exact.astype(jnp.bfloat16)
+                        low = (exact - high.astype(jnp.float32)).astype(jnp.bfloat16)
+                        lanes = slice(side * LANES, (side + 1) * LANES)
+                        for group in range(R_DEV // 16):
+                            rows = slice(16 * group, 16 * group + 16)
+                            here = slice((place * SUB_DEV + sub) * 16, (place * SUB_DEV + sub) * 16 + 16)
+                            factors[group, 2 * kind, here, lanes] = high[rows]
+                            factors[group, 2 * kind + 1, here, lanes] = low[rows]
+    copies[4].wait()
+    facet_products(lambda group, kind: own_factors[group, kind], rows_ref, outs, R_DEV, 0)
+
+
+def other_facet_kernel(rows_ref, factors, *rest):
+    earlier, outs = rest[:5], rest[5:]
+    core = lax.axis_index("row") % 2
+    for piece, out in zip(earlier, outs):
         for sub in range(SUB_DEV):
-            subgrid = (target * 2 + core) * SUB_DEV + sub
-            slot = (base - start_ref[subgrid]) & (total_rows - 1)
-            slot = jnp.where(slot > total_rows - R_DEV, slot - total_rows, slot)
-            slot = jnp.minimum(slot, SUB)
-            piece = padded[pl.ds(slot + R_DEV, R_DEV), :]
-            weights.append(jnp.where(slot + row_index < length_ref[subgrid], piece, 0.0))
-    for tile in range(R_DEV // 16):
-        rows = slice(16 * tile, 16 * tile + 16)
-        sums = [[None, None] for _ in weights]
-        for f in range(F):
-            real_in = rows_ref[0, f, rows, :].astype(jnp.float32)
-            imag_in = rows_ref[1, f, rows, :].astype(jnp.float32)
-            cos_f = cosines[rows, f : f + 1]
-            sin_f = sines[rows, f : f + 1]
-            real_part = cos_f * real_in - sin_f * imag_in
-            imag_part = cos_f * imag_in + sin_f * real_in
-            for entry, weight in zip(sums, weights):
-                w = jnp.broadcast_to(weight[rows, f : f + 1], (16, KC))
-                entry[0] = w * real_part if f == 0 else entry[0] + w * real_part
-                entry[1] = w * imag_part if f == 0 else entry[1] + w * imag_part
-        for place, entry in enumerate(sums):
-            out, sub = outs[place // SUB_DEV], place % SUB_DEV
-            if other:
-                first = pl.multiple_of(sub * CHIP + half * R_DEV + 16 * tile, 16)
-            else:
-                first = sub * R_DEV + 16 * tile
-            out[pl.ds(first, 16), :KC] = entry[0].astype(jnp.bfloat16)
-            out[pl.ds(first, 16), KC:] = entry[1].astype(jnp.bfloat16)
-    if other:
-        for piece, out in zip(earlier, outs):
-            for sub in range(SUB_DEV):
-                first = pl.multiple_of(sub * CHIP + core * R_DEV, R_DEV)
-                out[pl.ds(first, R_DEV), :] = piece[sub * R_DEV : (sub + 1) * R_DEV, :]
+            first = pl.multiple_of(sub * CHIP + core * R_DEV, R_DEV)
+            out[pl.ds(first, R_DEV), :] = piece[sub * R_DEV : (sub + 1) * R_DEV, :]
+    facet_products(lambda group, kind: factors[group, kind], rows_ref, outs, CHIP, (1 - core) * R_DEV)
 
 
 def taps(low, high, cell, table_row):
@@ -123,7 +189,7 @@
 def degrid_kernel(
     devices,
     per_dest,
-    start_ref,
+    shifts_ref,
     table_ref,
     transform_ref,
     own_ref,
@@ -139,8 +205,6 @@
     cells,
     gathered,
 ):
-    position = lax.axis_index("row")
-    chip = position // 2
     table = table_ref[...]
     near = table.astype(jnp.bfloat16).astype(jnp.float32)
     near_low, near_high = near[:, :LANES], near[:, LANES:]
@@ -165,8 +229,7 @@
     def one_block(block, carry):
         lanes = pl.ds(pl.multiple_of(block * BLOCK, BLOCK), BLOCK)
         for sub in range(SUB_DEV):
-            subgrid = position * SUB_DEV + sub
-            shift = start_ref[subgrid] - chip * CHIP
+            shift = jnp.concatenate([shifts_ref[sub, :1, :]] * (BLOCK // LANES), axis=1)
             cell_row = (row_ref[sub : sub + 1, lanes] + shift) & (SUB - 1)
             weights, tile = taps(near_low, near_high, cell_row, row_kernel_ref[sub : sub + 1, lanes])
             tile = tile & (SUB // 8 - 1)
@@ -232,26 +295,40 @@
     per_dest = slots // devices
     chunks = per_dest // LANES
     other_rows = lax.ppermute(facet_rows, "row", [(i, i ^ 1) for i in range(devices)])
-    small = pltpu.CompilerParams(vmem_limit_bytes=8 * 1024 * 1024)
-    tables = (range_start, range_length, facet_offset.reshape(1, F), window_table)
-    own_pieces = pl.pallas_call(
-        lambda *refs: facet_kernel(devices, *refs, other=False),
-        out_shape=[jax.ShapeDtypeStruct((SUB_DEV * R_DEV, 2 * KC), jnp.bfloat16)] * 5,
-        in_specs=[SMEM, SMEM, VMEM, VMEM, VMEM],
-        out_specs=[VMEM] * 5,
-        scratch_shapes=[pltpu.VMEM((SUB + 2 * R_DEV, F), jnp.float32)],
+    small = pltpu.CompilerParams(vmem_limit_bytes=12 * 1024 * 1024)
+    factors = jax.ShapeDtypeStruct((R_DEV // 16, 4, 5 * SUB_DEV * 16, 16 * F), jnp.bfloat16)
+    *own_pieces, other_factors, shifts = pl.pallas_call(
+        lambda *refs: own_facet_kernel(devices, *refs),
+        out_shape=[jax.ShapeDtypeStruct((SUB_DEV * R_DEV, 2 * KC), jnp.bfloat16)] * 5
+        + [factors, jax.ShapeDtypeStruct((SUB_DEV, 8, LANES), jnp.int32)],
+        in_specs=[HBM] * 5,
+        out_specs=[VMEM] * 7,
+        scratch_shapes=[
+            pltpu.SMEM(range_start.shape, jnp.int32),
+            pltpu.SMEM(range_length.shape, jnp.int32),
+            pltpu.VMEM((1, F), jnp.int32),
+            pltpu.VMEM(window_table.shape, jnp.float32),
+            pltpu.VMEM(facet_rows.shape, jnp.bfloat16),
+            pltpu.VMEM(factors.shape, jnp.bfloat16),
+            pltpu.VMEM((SUB + 2 * R_DEV, F), jnp.float32),
+            pltpu.SemaphoreType.DMA((5,)),
+        ],
         compiler_params=small,
         name="own_facet_sums",
-    )(*tables, facet_rows)
+    )(
+        *(
+            pltpu.with_memory_space_constraint(value, pltpu.HBM)
+            for value in (range_start, range_length, facet_offset.reshape(1, F), window_table, facet_rows)
+        )
+    )
     pieces = pl.pallas_call(
-        lambda *refs: facet_kernel(devices, *refs, other=True),
+        other_facet_kernel,
         out_shape=[jax.ShapeDtypeStruct((SUB_DEV * CHIP, 2 * KC), jnp.bfloat16)] * 5,
-        in_specs=[SMEM, SMEM] + [VMEM] * 8,
+        in_specs=[VMEM] * 7,
         out_specs=[VMEM] * 5,
-        scratch_shapes=[pltpu.VMEM((SUB + 2 * R_DEV, F), jnp.float32)],
         compiler_params=small,
         name="other_facet_sums",
-    )(*tables, other_rows, *own_pieces)
+    )(other_rows, other_factors, *own_pieces)
     came = []
     for shift, piece in zip(SHIFTS, pieces[1:]):
         pairs = [
@@ -264,7 +341,7 @@
     results = pl.pallas_call(
         lambda *refs: degrid_kernel(devices, per_dest, *refs),
         out_shape=jax.ShapeDtypeStruct((rows_out, LANES), jnp.bfloat16),
-        in_specs=[SMEM] + [VMEM] * 11,
+        in_specs=[VMEM] * 12,
         out_specs=VMEM,
         scratch_shapes=[
             pltpu.VMEM((SUB_DEV, 2 * SUB, SUB), jnp.bfloat16),
@@ -273,7 +350,7 @@
         compiler_params=pltpu.CompilerParams(vmem_limit_bytes=32 * 1024 * 1024),
         name="degrid",
     )(
-        range_start,
+        shifts,
         kernel_table.T,
         jnp.asarray(transform_table()),
         pieces[0],

time: 36.1 us -> 31.9 us (0.88)
  Pallas kernels: 10.1 us -> 8.26 us
  local copies, waits for them, and re-layouts: 1.86 us -> 0.04 us
  starting transfers between devices: 8.67 us -> 8.15 us
    unnamed x22 -> x12, local copies, waits for them, and re-layouts: 1.86 us -> 0.04 us
    pallas_call x2, Pallas kernels: 3.39 us -> 2.04 us  [the longest x1 1.69 us: local(): pl.pallas_call(lambda *refs: own_facet_kernel(devices, *refs), out_shape=...]
    pallas_call x1, Pallas kernels: 6.03 us -> 5.53 us  [local(): pl.pallas_call(lambda *refs: degrid_kernel(devices, per_dest, *refs), out...]
    ppermute x4, starting transfers between devices: 8.15 us -> 7.7 us  [local(): came.append(lax.ppermute(piece, 'row', pairs))]
  transfers between devices with their start and end apart: 5 -> 5, of which waited for: 3 -> 4; matrix products, arithmetic and copies ran while one was open for 0% -> 0% of each run, Pallas kernels for 5% -> 5%
where the time goes in v2:
time: 31.9 us; the launch traced here: 31.7 us
  blocking collectives  12.2 us (38%)
  Pallas kernels  8.26 us (26%)
  starting transfers between devices  8.15 us (26%)
  waiting for transfers between devices  2.96 us (9%)
    all_to_all x1, blocking collectives, local(): lax.all_to_all(results.reshape(devices, 4 * chunks, LANES), 'row', split_...  12.2 us
    ppermute x4, starting transfers between devices, local(): came.append(lax.ppermute(piece, 'row', pairs))  7.7 us
    pallas_call x1, Pallas kernels, local(): pl.pallas_call(lambda *refs: degrid_kernel(devices, per_dest, *refs), out...  5.53 us
    ppermute x4, waiting for transfers between devices, local(): came.append(lax.ppermute(piece, 'row', pairs))  2.96 us
    pallas_call x1, Pallas kernels, local(): pl.pallas_call(lambda *refs: own_facet_kernel(devices, *refs), out_shape=...  1.69 us
    pallas_call x1, Pallas kernels, local(): pl.pallas_call(lambda *refs: place_kernel(devices, chunks, *refs), out_sh...  0.69 us
  transfers between devices with their start and end apart: 5, of which 4 were waited for; matrix products, arithmetic and copies ran while one was open for 0% of the time, Pallas kernels for 5%

profile of v2, /device:TPU:0, one launch (start us, length us, event | category | flops | bytes accessed | tf_op | source)
XLA Modules:
  0.0 31.7 jit_solution(8790304329825333435)
XLA Ops:
  0.0 0.5 %collective-permute-start = (bf16[2,16,32,128]{3,2,1,0:T(8,128)(2,1)}, bf16[2,16,32,128]{3,2,1,0:T(8,128)(2,1)S(1)}, u32[]{:S(2)}, u32[]{:S(2)}) collective-permute-start(bf16[2,16,32,128]{3,2,1,0:T(8,128)(2,1)} %refs_4_.1), channel_id=1, source_target_pairs={{0,1},{1,0},{2,3},{3,2},{4,5},{5,4},{6,7},{7,6},{8,9},{9,8},{10,11... | collective-permute-start | bytes 786440 | tf_op jit(solution)/shard_map/ppermute | solution.py:297
  0.5 1.7 %own_facet_sums.1 = (bf16[64,256]{1,0:T(8,128)(2,1)S(1)}, bf16[64,256]{1,0:T(8,128)(2,1)S(1)}, bf16[64,256]{1,0:T(8,128)(2,1)S(1)}, bf16[64,256]{1,0:T(8,128)(2,...) custom-call(s32[32]{0:T(128)} %refs_0_.1, s32[32]{0:T(128)} %refs_1_.1, ...), custom_call_target="tpu_custom_call" | custom-call | tf_op jit(solution)/shard_map/own_facet_sums/pallas_call | solution.py:300
  2.2 0.0 collective-permute-done.rows_ref
  2.2 0.0 copy-start
  2.2 0.0 copy-start.1
  2.2 0.0 copy-start.2
  2.2 0.0 copy-start.3
  2.2 0.0 copy-start.4
  2.2 0.3 %other_facet_sums.1 = (bf16[128,256]{1,0:T(8,128)(2,1)S(1)}, bf16[128,256]{1,0:T(8,128)(2,1)S(1)}, bf16[128,256]{1,0:T(8,128)(2,1)S(1)}, bf16[128,256]{1,0:T(8,128)(2,1)S(1)}, bf16[128,256]{1,0:T(8,128)(2,1)S(1)}) custom-call(bf16[2,16,32,128]{3,2,1,0:T(8,128)(2,1)S(1)} %collective-permute-done.rows_ref, ...), custom_call_target="tpu_custom_call" | custom-call | tf_op jit(solution)/shard_map/other_facet_sums/pallas_call | solution.py:324
  2.6 0.0 copy-start.5
  2.6 2.6 %collective-permute-start.1 = (bf16[128,256]{1,0:T(8,128)(2,1)S(1)}, bf16[128,256]{1,0:T(8,128)(2,1)S(1)}, u32[]{:S(2)}, u32[]{:S(2)}) collective-permute-start(bf16[128,256]{1,0:T(8,128)(2,1)S(1)} %get-tuple-element.25), channel_id=1, source_target_pairs={{0,2},{1,3},{2,4},{3,5},{4,6},{5,7},{6,8},{7,9},{8,10},{9,11},{10,... | collective-permute-start | bytes 196616 | tf_op jit(solution)/shard_map/ppermute | solution.py:339
  5.2 1.6 %collective-permute-start.2 = (bf16[128,256]{1,0:T(8,128)(2,1)S(1)}, bf16[128,256]{1,0:T(8,128)(2,1)S(1)}, u32[]{:S(2)}, u32[]{:S(2)}) collective-permute-start(bf16[128,256]{1,0:T(8,128)(2,1)S(1)} %get-tuple-element.26), channel_id=1, source_target_pairs={{0,4},{1,5},{2,6},{3,7},{4,8},{5,9},{6,10},{7,11},{8,12},{9,13},{1... | collective-permute-start | bytes 196616 | tf_op jit(solution)/shard_map/ppermute | solution.py:339
  6.7 2.2 %collective-permute-start.3 = (bf16[128,256]{1,0:T(8,128)(2,1)S(1)}, bf16[128,256]{1,0:T(8,128)(2,1)S(1)}, u32[]{:S(2)}, u32[]{:S(2)}) collective-permute-start(bf16[128,256]{1,0:T(8,128)(2,1)S(1)} %get-tuple-element.27), channel_id=1, source_target_pairs={{0,12},{1,13},{2,14},{3,15},{4,0},{5,1},{6,2},{7,3},{8,4},{9,5},{1... | collective-permute-start | bytes 196616 | tf_op jit(solution)/shard_map/ppermute | solution.py:339
  9.0 1.3 %collective-permute-start.4 = (bf16[128,256]{1,0:T(8,128)(2,1)S(1)}, bf16[128,256]{1,0:T(8,128)(2,1)S(1)}, u32[]{:S(2)}, u32[]{:S(2)}) collective-permute-start(bf16[128,256]{1,0:T(8,128)(2,1)S(1)} %get-tuple-element.28), channel_id=1, source_target_pairs={{0,14},{1,15},{2,0},{3,1},{4,2},{5,3},{6,4},{7,5},{8,6},{9,7},{10,... | collective-permute-start | bytes 196616 | tf_op jit(solution)/shard_map/ppermute | solution.py:339
  10.3 0.9 %collective-permute-done.1.refs_4_ = bf16[128,256]{1,0:T(8,128)(2,1)S(1)} collective-permute-done((bf16[128,256]{1,0:T(8,128)(2,1)S(1)}, bf16[128,256]{1,0:T(8,128)(2,1)S(1)}, u32[]{:S(2)}, u32[]{:S(2)}) %collective-permute-start.1) | collective-permute-done | bytes 65568 | tf_op jit(solution)/shard_map/ppermute | solution.py:339
  11.2 0.2 collective-permute-done.2.refs_5_
  11.4 0.7 %collective-permute-done.3.refs_6_ = bf16[128,256]{1,0:T(8,128)(2,1)S(1)} collective-permute-done((bf16[128,256]{1,0:T(8,128)(2,1)S(1)}, bf16[128,256]{1,0:T(8,128)(2,1)S(1)}, u32[]{:S(2)}, u32[]{:S(2)}) %collective-permute-start.3) | collective-permute-done | bytes 65568 | tf_op jit(solution)/shard_map/ppermute | solution.py:339
  12.1 1.2 %collective-permute-done.4.refs_7_ = bf16[128,256]{1,0:T(8,128)(2,1)S(1)} collective-permute-done((bf16[128,256]{1,0:T(8,128)(2,1)S(1)}, bf16[128,256]{1,0:T(8,128)(2,1)S(1)}, u32[]{:S(2)}, u32[]{:S(2)}) %collective-permute-start.4) | collective-permute-done | bytes 65568 | tf_op jit(solution)/shard_map/ppermute | solution.py:339
  13.2 0.0 copy-done
  13.3 0.0 copy-done.1
  13.3 0.0 copy-done.2
  13.3 0.0 copy-done.3
  13.3 0.0 copy-done.4
  13.3 0.0 copy-done.5
  13.3 5.5 %degrid.1 = bf16[256,128]{1,0:T(8,128)(2,1)S(1)} custom-call(s32[2,8,128]{2,1,0:T(8,128)S(1)} %get-tuple-element.17.refs_0_, f32[8,256]{1,0:T(8,128)S(1)} %bitcast.6, bf16[512,256]{1,0:T(8,128)(2,1)S(1)} %copy-done, bf16[128,256]{1,0:T(8,128)(2,1)S(1)} %get-tuple-element.24.refs_3_, bf16[128,256]{1,0:T(8,128)(2,1)S(1)} %collective-permute-done.1.refs_4_, ...), custom_call_target="tpu_custom_call" | custom-call | tf_op jit(solution)/shard_map/degrid/pallas_call | solution.py:341
  18.8 12.2 %all_to_all.5 = bf16[16,16,128]{2,1,0:T(8,128)(2,1)S(1)} all-to-all(bf16[16,16,128]{2,1,0:T(8,128)(2,1)S(1)} %bitcast.4), channel_id=1, replica_groups=mesh['grp'=2,'row'=16] {'row'}, dimensions={0} | all-to-all | bytes 131072 | tf_op jit(solution)/shard_map/all_to_all | solution.py:363
  31.0 0.7 %place.1 = f32[2,32,512]{2,1,0:T(8,128)} custom-call(bf16[256,128]{1,0:T(8,128)(2,1)S(1)} %bitcast.5), custom_call_target="tpu_custom_call" | custom-call | tf_op jit(solution)/shard_map/place/pallas_call | solution.py:366
Async XLA Ops:
  0.0 2.2 %collective-permute-start = (bf16[2,16,32,128]{3,2,1,0:T(8,128)(2,1)}, bf16[2,16,32,128]{3,2,1,0:T(8,128)(2,1)S(1)}, u32[]{:S(2)}, u32[]{:S(2)}) collective-permute-start(bf16[2,16,32,128]{3,2,1,0:T(8,128)(2,1)} %refs_4_.1), channel_id=1, source_target_pairs={{0,1},{1,0},{2,3},{3,2},{4,5},{5,4},{6,7},{7,6},{8,9},{9,8},{10,11... | collective-permute-start | bytes 786440 | tf_op jit(solution)/shard_map/ppermute | solution.py:297
  2.2 11.1 %copy-start = (bf16[512,256]{1,0:T(8,128)(2,1)S(1)}, bf16[512,256]{1,0:T(8,128)(2,1)}, u32[]{:S(2)}) copy-start(bf16[512,256]{1,0:T(8,128)(2,1)} %constant.2.clone.refs_2_) | copy-start | bytes 786436
  2.2 11.1 %copy-start.1 = (s32[2,8192]{1,0:T(2,128)S(1)}, s32[2,8192]{1,0:T(2,128)}, u32[]{:S(2)}) copy-start(s32[2,8192]{1,0:T(2,128)} %refs_8_.1) | copy-start | bytes 196612
  2.2 11.1 %copy-start.2 = (s32[2,8192]{1,0:T(2,128)S(1)}, s32[2,8192]{1,0:T(2,128)}, u32[]{:S(2)}) copy-start(s32[2,8192]{1,0:T(2,128)} %refs_9_.1) | copy-start | bytes 196612
  2.2 11.1 %copy-start.3 = (s32[2,8192]{1,0:T(2,128)S(1)}, s32[2,8192]{1,0:T(2,128)}, u32[]{:S(2)}) copy-start(s32[2,8192]{1,0:T(2,128)} %refs_10_.1) | copy-start | bytes 196612
  2.2 11.1 %copy-start.4 = (s32[2,8192]{1,0:T(2,128)S(1)}, s32[2,8192]{1,0:T(2,128)}, u32[]{:S(2)}) copy-start(s32[2,8192]{1,0:T(2,128)} %refs_11_.1) | copy-start | bytes 196612
  2.6 10.7 %copy-start.5 = (f32[256,8]{0,1:T(8,128)S(1)}, f32[256,8]{0,1:T(8,128)}, u32[]{:S(2)}) copy-start(f32[256,8]{0,1:T(8,128)} %param.16) | copy-start | bytes 24580
  2.6 8.6 %collective-permute-start.1 = (bf16[128,256]{1,0:T(8,128)(2,1)S(1)}, bf16[128,256]{1,0:T(8,128)(2,1)S(1)}, u32[]{:S(2)}, u32[]{:S(2)}) collective-permute-start(bf16[128,256]{1,0:T(8,128)(2,1)S(1)} %get-tuple-element.25), channel_id=1, source_target_pairs={{0,2},{1,3},{2,4},{3,5},{4,6},{5,7},{6,8},{7,9},{8,10},{9,11},{10,... | collective-permute-start | bytes 196616 | tf_op jit(solution)/shard_map/ppermute | solution.py:339
  5.2 6.2 %collective-permute-start.2 = (bf16[128,256]{1,0:T(8,128)(2,1)S(1)}, bf16[128,256]{1,0:T(8,128)(2,1)S(1)}, u32[]{:S(2)}, u32[]{:S(2)}) collective-permute-start(bf16[128,256]{1,0:T(8,128)(2,1)S(1)} %get-tuple-element.26), channel_id=1, source_target_pairs={{0,4},{1,5},{2,6},{3,7},{4,8},{5,9},{6,10},{7,11},{8,12},{9,13},{1... | collective-permute-start | bytes 196616 | tf_op jit(solution)/shard_map/ppermute | solution.py:339
  6.7 5.3 %collective-permute-start.3 = (bf16[128,256]{1,0:T(8,128)(2,1)S(1)}, bf16[128,256]{1,0:T(8,128)(2,1)S(1)}, u32[]{:S(2)}, u32[]{:S(2)}) collective-permute-start(bf16[128,256]{1,0:T(8,128)(2,1)S(1)} %get-tuple-element.27), channel_id=1, source_target_pairs={{0,12},{1,13},{2,14},{3,15},{4,0},{5,1},{6,2},{7,3},{8,4},{9,5},{1... | collective-permute-start | bytes 196616 | tf_op jit(solution)/shard_map/ppermute | solution.py:339
  9.0 4.3 %collective-permute-start.4 = (bf16[128,256]{1,0:T(8,128)(2,1)S(1)}, bf16[128,256]{1,0:T(8,128)(2,1)S(1)}, u32[]{:S(2)}, u32[]{:S(2)}) collective-permute-start(bf16[128,256]{1,0:T(8,128)(2,1)S(1)} %get-tuple-element.28), channel_id=1, source_target_pairs={{0,14},{1,15},{2,0},{3,1},{4,2},{5,3},{6,4},{7,5},{8,6},{9,7},{10,... | collective-permute-start | bytes 196616 | tf_op jit(solution)/shard_map/ppermute | solution.py:339

commit v3 on v2

--- a/solution.py
+++ b/solution.py
@@ -19,11 +19,19 @@
 LANES = 128
 BLOCK = 1024
 UNROLL = 4
+PART = 512
+PART_UNROLL = 8
 
 TWO_PI = 2.0 * math.pi
 
 VMEM = pl.BlockSpec(memory_space=pltpu.VMEM)
 HBM = pl.BlockSpec(memory_space=pltpu.HBM)
+
+
+def turned_rows():
+    wave = np.arange(KC)
+    place = wave // 8 * 16 + wave % 8
+    return np.concatenate([place, place + 8])
 
 
 def transform_table():
@@ -31,14 +39,14 @@
     jcol = np.arange(SUB)
     angles = np.float32(TWO_PI) * (kcol[:, None] * jcol[None, :] % SUB).astype(np.float32) / np.float32(SUB)
     scale = np.float32(1.0 / math.sqrt(KC))
-    real_part = (np.cos(angles) * scale).astype(jnp.bfloat16)
-    imag_part = (np.sin(angles) * scale).astype(jnp.bfloat16)
-    upper = np.concatenate([real_part, imag_part], axis=1)
-    lower = np.concatenate([-imag_part, real_part], axis=1)
-    return np.ascontiguousarray(np.concatenate([upper, lower], axis=0).T)
+    parts = np.concatenate([np.cos(angles) * scale, np.sin(angles) * scale], axis=0).astype(jnp.bfloat16)
+    table = np.zeros_like(parts)
+    table[turned_rows()] = parts
+    return table
 
 
 SHIFTS = (1, 2, -2, -1)
+LATER = 6
 
 
 def facet_products(factors, rows_ref, outs, half_step, first_row):
@@ -74,8 +82,9 @@
     rows_hbm,
     *rest,
 ):
-    outs, other_factors, shifts = rest[:5], rest[5], rest[6]
-    start, length, offset, window, rows_ref, own_factors, padded, sems = rest[7:]
+    later_hbm, rest = rest[:LATER], rest[LATER:]
+    outs, other_factors, shifts, later = rest[:5], rest[5], rest[6], rest[7 : 7 + LATER]
+    start, length, offset, window, rows_ref, own_factors, padded, sems = rest[7 + LATER :]
     copies = [
         pltpu.make_async_copy(source, target, sems.at[number])
         for number, (source, target) in enumerate(
@@ -85,6 +94,7 @@
                 (offset_hbm, offset),
                 (window_hbm, window),
                 (rows_hbm, rows_ref),
+                *zip(later_hbm, later),
             )
         )
     ]
@@ -154,10 +164,13 @@
                             factors[group, 2 * kind + 1, here, lanes] = low[rows]
     copies[4].wait()
     facet_products(lambda group, kind: own_factors[group, kind], rows_ref, outs, R_DEV, 0)
-
-
-def other_facet_kernel(rows_ref, factors, *rest):
-    earlier, outs = rest[:5], rest[5:]
+    for copy in copies[5:]:
+        copy.wait()
+
+
+def other_facet_kernel(rows_ref, factors, shifts, *rest):
+    earlier, outs, shifts_out = rest[:5], rest[5:10], rest[10]
+    shifts_out[...] = shifts[...]
     core = lax.axis_index("row") % 2
     for piece, out in zip(earlier, outs):
         for sub in range(SUB_DEV):
@@ -166,7 +179,7 @@
     facet_products(lambda group, kind: factors[group, kind], rows_ref, outs, CHIP, (1 - core) * R_DEV)
 
 
-def taps(low, high, cell, table_row):
+def spread(low, high, cell, table_row):
     count = cell.shape[1]
     cell = jnp.broadcast_to(cell, (SUPPORT, count))
     table_row = jnp.broadcast_to(table_row, (SUPPORT, count))
@@ -182,33 +195,57 @@
         turned = pltpu.roll(weights, 1 << bit, axis=0)
         weights = jnp.where((cell & (1 << bit)) != 0, turned, weights)
     sublane = lax.broadcasted_iota(jnp.int32, (SUPPORT, count), 0)
-    tile = (cell >> 3) + jnp.where(sublane < (cell & 7), 1, 0)
-    return weights, tile
-
-
-def degrid_kernel(
-    devices,
-    per_dest,
+    tile = ((cell >> 3) + jnp.where(sublane < (cell & 7), 1, 0)) & (SUB // 8 - 1)
+    odd = (tile & 1) != 0
+    pair = (tile >> 1).astype(jnp.float32)
+    pairs = jnp.concatenate([jnp.where(odd, -1.0, pair), jnp.where(odd, pair, -1.0)], axis=0).astype(jnp.bfloat16)
+    both = jnp.concatenate([weights, weights], axis=0).astype(jnp.bfloat16)
+    zero = jnp.zeros_like(both)
+    return jnp.concatenate([jnp.where(pairs == jnp.bfloat16(t), both, zero) for t in range(SUB // 16)], axis=0)
+
+
+def spread_kernel(
     shifts_ref,
     table_ref,
     transform_ref,
+    row_ref,
+    column_ref,
+    row_kernel_ref,
+    column_kernel_ref,
+    row_spread,
+    column_waves,
+):
+    low, high = table_ref[:, :LANES], table_ref[:, LANES:]
+
+    def one_block(block, carry):
+        lanes = pl.ds(pl.multiple_of(block * BLOCK, BLOCK), BLOCK)
+        for sub in range(SUB_DEV):
+            shift = jnp.concatenate([shifts_ref[sub, :1, :]] * (BLOCK // LANES), axis=1)
+            cell_row = (row_ref[sub : sub + 1, lanes] + shift) & (SUB - 1)
+            row_spread[sub, :, lanes] = spread(low, high, cell_row, row_kernel_ref[sub : sub + 1, lanes])
+            columns = spread(low, high, column_ref[sub : sub + 1, lanes], column_kernel_ref[sub : sub + 1, lanes])
+            column_waves[sub, :, lanes] = jnp.dot(transform_ref[...], columns, preferred_element_type=jnp.float32)
+        return carry
+
+    lax.fori_loop(0, row_ref.shape[1] // BLOCK, one_block, 0, unroll=UNROLL)
+
+
+def degrid_kernel(
+    per_dest,
     own_ref,
     below_ref,
     far_below_ref,
     far_above_ref,
     above_ref,
-    row_ref,
-    column_ref,
-    row_kernel_ref,
-    column_kernel_ref,
+    row_spread,
+    column_waves,
     out_ref,
-    cells,
+    waves,
     gathered,
 ):
-    table = table_ref[...]
-    near = table.astype(jnp.bfloat16).astype(jnp.float32)
-    near_low, near_high = near[:, :LANES], near[:, LANES:]
-    table_low, table_high = table[:, :LANES], table[:, LANES:]
+    wave = lax.broadcasted_iota(jnp.int32, (2 * KC, 2 * KC), 1)
+    place = ((wave & (KC - 1)) >> 3) * 16 + (wave & 7) + jnp.where(wave < KC, 0, 8)
+    turn = (lax.broadcasted_iota(jnp.int32, (2 * KC, 2 * KC), 0) == place).astype(jnp.float32).astype(jnp.bfloat16)
     for sub in range(SUB_DEV):
         rows = slice(sub * CHIP, sub * CHIP + CHIP)
         summed = jnp.concatenate(
@@ -220,51 +257,35 @@
             ],
             axis=0,
         )
-        cells[sub] = lax.dot_general(
-            transform_ref[...], summed, (((1,), (1,)), ((), ())), preferred_element_type=jnp.float32
+        waves[sub] = lax.dot_general(
+            turn, summed, (((1,), (1,)), ((), ())), preferred_element_type=jnp.float32
         ).astype(jnp.bfloat16)
-
     chunks = per_dest // LANES
 
     def one_block(block, carry):
-        lanes = pl.ds(pl.multiple_of(block * BLOCK, BLOCK), BLOCK)
+        lanes = pl.ds(pl.multiple_of(block * PART, PART), PART)
         for sub in range(SUB_DEV):
-            shift = jnp.concatenate([shifts_ref[sub, :1, :]] * (BLOCK // LANES), axis=1)
-            cell_row = (row_ref[sub : sub + 1, lanes] + shift) & (SUB - 1)
-            weights, tile = taps(near_low, near_high, cell_row, row_kernel_ref[sub : sub + 1, lanes])
-            tile = tile & (SUB // 8 - 1)
-            odd = (tile & 1) != 0
-            pair = (tile >> 1).astype(jnp.float32)
-            pairs = jnp.concatenate(
-                [jnp.where(odd, -1.0, pair), jnp.where(odd, pair, -1.0)], axis=0
-            ).astype(jnp.bfloat16)
-            both = jnp.concatenate([weights, weights], axis=0).astype(jnp.bfloat16)
-            zero = jnp.zeros_like(both)
-            spread = jnp.concatenate(
-                [jnp.where(pairs == jnp.bfloat16(t), both, zero) for t in range(SUB // 16)], axis=0
-            )
-            along = jnp.dot(cells[sub], spread, preferred_element_type=jnp.float32)
-            weights, tile = taps(
-                table_low, table_high, column_ref[sub : sub + 1, lanes], column_kernel_ref[sub : sub + 1, lanes]
-            )
-            real_part = along[:8]
-            imag_part = along[SUB : SUB + 8]
-            for t in range(1, SUB // 8):
-                here = tile == t
-                real_part = jnp.where(here, along[8 * t : 8 * t + 8], real_part)
-                imag_part = jnp.where(here, along[SUB + 8 * t : SUB + 8 * t + 8], imag_part)
-            sums = [
-                jnp.sum(weights * real_part, axis=0, keepdims=True),
-                jnp.sum(weights * imag_part, axis=0, keepdims=True),
-            ]
-            first = block * (BLOCK // LANES * 4)
+            along = jnp.dot(waves[sub], row_spread[sub, :, lanes], preferred_element_type=jnp.float32)
+            sums = [None, None]
+            for t in range(KC // 8):
+                real = slice(16 * t, 16 * t + 8)
+                imag = slice(16 * t + 8, 16 * t + 16)
+                real_wave = column_waves[sub, real, lanes]
+                imag_wave = column_waves[sub, imag, lanes]
+                terms = (
+                    along[real] * real_wave - along[imag] * imag_wave,
+                    along[real] * imag_wave + along[imag] * real_wave,
+                )
+                sums = [term if t == 0 else total + term for total, term in zip(sums, terms)]
+            first = block * (PART // LANES * 4)
             for part in range(2):
-                for place in range(BLOCK // LANES):
+                total = jnp.sum(sums[part], axis=0, keepdims=True)
+                for place in range(PART // LANES):
                     row = place // chunks * 4 * chunks + (sub * 2 + part) * chunks + place % chunks
-                    gathered[pl.ds(first + row, 1), :] = sums[part][:, place * LANES : (place + 1) * LANES]
+                    gathered[pl.ds(first + row, 1), :] = total[:, place * LANES : (place + 1) * LANES]
         return carry
 
-    lax.fori_loop(0, row_ref.shape[1] // BLOCK, one_block, 0, unroll=UNROLL)
+    lax.fori_loop(0, row_spread.shape[2] // PART, one_block, 0, unroll=PART_UNROLL)
     out_ref[...] = gathered[...].astype(jnp.bfloat16)
 
 
@@ -297,12 +318,14 @@
     other_rows = lax.ppermute(facet_rows, "row", [(i, i ^ 1) for i in range(devices)])
     small = pltpu.CompilerParams(vmem_limit_bytes=12 * 1024 * 1024)
     factors = jax.ShapeDtypeStruct((R_DEV // 16, 4, 5 * SUB_DEV * 16, 16 * F), jnp.bfloat16)
-    *own_pieces, other_factors, shifts = pl.pallas_call(
+    later = (kernel_table.T, jnp.asarray(transform_table()), cell_row, cell_column, kernel_row, kernel_column)
+    *own_pieces, other_factors, shifts, table, transform, rows, columns, row_kernels, column_kernels = pl.pallas_call(
         lambda *refs: own_facet_kernel(devices, *refs),
         out_shape=[jax.ShapeDtypeStruct((SUB_DEV * R_DEV, 2 * KC), jnp.bfloat16)] * 5
-        + [factors, jax.ShapeDtypeStruct((SUB_DEV, 8, LANES), jnp.int32)],
-        in_specs=[HBM] * 5,
-        out_specs=[VMEM] * 7,
+        + [factors, jax.ShapeDtypeStruct((SUB_DEV, 8, LANES), jnp.int32)]
+        + [jax.ShapeDtypeStruct(value.shape, value.dtype) for value in later],
+        in_specs=[HBM] * (5 + LATER),
+        out_specs=[VMEM] * (7 + LATER),
         scratch_shapes=[
             pltpu.SMEM(range_start.shape, jnp.int32),
             pltpu.SMEM(range_length.shape, jnp.int32),
@@ -311,24 +334,25 @@
             pltpu.VMEM(facet_rows.shape, jnp.bfloat16),
             pltpu.VMEM(factors.shape, jnp.bfloat16),
             pltpu.VMEM((SUB + 2 * R_DEV, F), jnp.float32),
-            pltpu.SemaphoreType.DMA((5,)),
+            pltpu.SemaphoreType.DMA((5 + LATER,)),
         ],
         compiler_params=small,
         name="own_facet_sums",
     )(
         *(
             pltpu.with_memory_space_constraint(value, pltpu.HBM)
-            for value in (range_start, range_length, facet_offset.reshape(1, F), window_table, facet_rows)
+            for value in (range_start, range_length, facet_offset.reshape(1, F), window_table, facet_rows, *later)
         )
     )
-    pieces = pl.pallas_call(
+    *pieces, shifts = pl.pallas_call(
         other_facet_kernel,
-        out_shape=[jax.ShapeDtypeStruct((SUB_DEV * CHIP, 2 * KC), jnp.bfloat16)] * 5,
-        in_specs=[VMEM] * 7,
-        out_specs=[VMEM] * 5,
+        out_shape=[jax.ShapeDtypeStruct((SUB_DEV * CHIP, 2 * KC), jnp.bfloat16)] * 5
+        + [jax.ShapeDtypeStruct((SUB_DEV, 8, LANES), jnp.int32)],
+        in_specs=[VMEM] * 8,
+        out_specs=[VMEM] * 6,
         compiler_params=small,
         name="other_facet_sums",
-    )(other_rows, other_factors, *own_pieces)
+    )(other_rows, other_factors, shifts, *own_pieces)
     came = []
     for shift, piece in zip(SHIFTS, pieces[1:]):
         pairs = [
@@ -338,28 +362,33 @@
         ]
         came.append(lax.ppermute(piece, "row", pairs))
     rows_out = devices * 4 * chunks
+    spread_shape = (SUB_DEV, SUB, slots)
+    row_spread, column_waves = pl.pallas_call(
+        spread_kernel,
+        out_shape=[
+            jax.ShapeDtypeStruct(spread_shape, jnp.bfloat16),
+            jax.ShapeDtypeStruct(spread_shape, jnp.float32),
+        ],
+        in_specs=[VMEM] * 7,
+        out_specs=[VMEM] * 2,
+        compiler_params=small,
+        cost_estimate=pl.CostEstimate(
+            flops=2 * SUB_DEV * SUB * 2 * KC * slots, bytes_accessed=6 * SUB_DEV * SUB * slots, transcendentals=0
+        ),
+        name="spread",
+    )(shifts, table, transform, rows, columns, row_kernels, column_kernels)
     results = pl.pallas_call(
-        lambda *refs: degrid_kernel(devices, per_dest, *refs),
+        lambda *refs: degrid_kernel(per_dest, *refs),
         out_shape=jax.ShapeDtypeStruct((rows_out, LANES), jnp.bfloat16),
-        in_specs=[VMEM] * 12,
+        in_specs=[VMEM] * 7,
         out_specs=VMEM,
         scratch_shapes=[
-            pltpu.VMEM((SUB_DEV, 2 * SUB, SUB), jnp.bfloat16),
+            pltpu.VMEM((SUB_DEV, 2 * KC, SUB), jnp.bfloat16),
             pltpu.VMEM((rows_out, LANES), jnp.float32),
         ],
-        compiler_params=pltpu.CompilerParams(vmem_limit_bytes=32 * 1024 * 1024),
+        compiler_params=small,
         name="degrid",
-    )(
-        shifts,
-        kernel_table.T,
-        jnp.asarray(transform_table()),
-        pieces[0],
-        *came,
-        cell_row,
-        cell_column,
-        kernel_row,
-        kernel_column,
-    )
+    )(pieces[0], *came, row_spread, column_waves)
     received = lax.all_to_all(
         results.reshape(devices, 4 * chunks, LANES), "row", split_axis=0, concat_axis=0, tiled=True
     )

time: 31.9 us -> 30.1 us (0.944)
  waiting for transfers between devices: 2.96 us -> 0.01 us
  Pallas kernels: 8.26 us -> 10.6 us
  blocking collectives: 12.2 us -> 11 us
    ppermute x4, waiting for transfers between devices: 2.96 us -> 0.01 us  [local(): came.append(lax.ppermute(piece, 'row', pairs))]
    pallas_call x1 -> x2, Pallas kernels: 5.53 us -> 7.85 us  [the longest x1 4.07 us: local(): pl.pallas_call(spread_kernel, out_shape=[jax.ShapeDtypeStruct(spread_shap...]
    all_to_all x1, blocking collectives: 12.2 us -> 11 us  [local(): lax.all_to_all(results.reshape(devices, 4 * chunks, LANES), 'row', split_...]
  transfers between devices with their start and end apart: 5 -> 5, of which waited for: 4 -> 0; matrix products, arithmetic and copies ran while one was open for 0% -> 0% of each run, Pallas kernels for 5% -> 19%
where the time goes in v3:
time: 30.1 us; the launch traced here: 29.9 us
  blocking collectives  11 us (37%)
  Pallas kernels  10.6 us (35%)
  starting transfers between devices  8.16 us (27%)
    all_to_all x1, blocking collectives, local(): lax.all_to_all(results.reshape(devices, 4 * chunks, LANES), 'row', split_...  11 us
    ppermute x4, starting transfers between devices, local(): came.append(lax.ppermute(piece, 'row', pairs))  7.71 us
    pallas_call x1, Pallas kernels, local(): pl.pallas_call(spread_kernel, out_shape=[jax.ShapeDtypeStruct(spread_shap...  4.07 us
    pallas_call x1, Pallas kernels, local(): pl.pallas_call(lambda *refs: degrid_kernel(per_dest, *refs), out_shape=ja...  3.78 us
    pallas_call x1, Pallas kernels, local(): pl.pallas_call(lambda *refs: own_facet_kernel(devices, *refs), out_shape=...  1.76 us
    pallas_call x1, Pallas kernels, local(): pl.pallas_call(lambda *refs: place_kernel(devices, chunks, *refs), out_sh...  0.69 us
  transfers between devices with their start and end apart: 5, of which 0 were waited for; matrix products, arithmetic and copies ran while one was open for 0% of the time, Pallas kernels for 19%

profile of v3, /device:TPU:0, one launch (start us, length us, event | category | flops | bytes accessed | tf_op | source)
XLA Modules:
  0.0 29.9 jit_solution(2963166644914936879)
XLA Ops:
  0.0 0.5 %collective-permute-start = (bf16[2,16,32,128]{3,2,1,0:T(8,128)(2,1)}, bf16[2,16,32,128]{3,2,1,0:T(8,128)(2,1)S(1)}, u32[]{:S(2)}, u32[]{:S(2)}) collective-permute-start(bf16[2,16,32,128]{3,2,1,0:T(8,128)(2,1)} %refs_4_.1), channel_id=1, source_target_pairs={{0,1},{1,0},{2,3},{3,2},{4,5},{5,4},{6,7},{7,6},{8,9},{9,8},{10,11... | collective-permute-start | bytes 786440 | tf_op jit(solution)/shard_map/ppermute | solution.py:318
  0.5 1.8 %own_facet_sums.1 = (bf16[64,256]{1,0:T(8,128)(2,1)S(1)}, bf16[64,256]{1,0:T(8,128)(2,1)S(1)}, bf16[64,256]{1,0:T(8,128)(2,1)S(1)}, bf16[64,256]{1,0:T(8,128)(2,...) custom-call(s32[32]{0:T(128)} %refs_0_.1, ...), custom_call_target="tpu_custom_call" | custom-call | tf_op jit(solution)/shard_map/own_facet_sums/pallas_call | solution.py:322
  2.2 0.0 collective-permute-done.rows_ref
  2.2 0.3 %other_facet_sums.1 = (bf16[128,256]{1,0:T(8,128)(2,1)S(1)}, bf16[128,256]{1,0:T(8,128)(2,1)S(1)}, bf16[128,256]{1,0:T(8,128)(2,1)S(1)}, bf16[128,256]{1,0:T(8,1...) custom-call(bf16[2,16,32,128]{3,2,1,0:T(8,128)(2,1)S(1)} %collective-permute-done.rows_ref, ...), custom_call_target="tpu_custom_call" | custom-call | tf_op jit(solution)/shard_map/other_facet_sums/pallas_call | solution.py:347
  2.6 2.6 %collective-permute-start.1 = (bf16[128,256]{1,0:T(8,128)(2,1)S(1)}, bf16[128,256]{1,0:T(8,128)(2,1)S(1)}, u32[]{:S(2)}, u32[]{:S(2)}) collective-permute-start(bf16[128,256]{1,0:T(8,128)(2,1)S(1)} %get-tuple-element.34), channel_id=1, source_target_pairs={{0,2},{1,3},{2,4},{3,5},{4,6},{5,7},{6,8},{7,9},{8,10},{9,11},{10,... | collective-permute-start | bytes 196616 | tf_op jit(solution)/shard_map/ppermute | solution.py:363
  5.1 1.6 %collective-permute-start.2 = (bf16[128,256]{1,0:T(8,128)(2,1)S(1)}, bf16[128,256]{1,0:T(8,128)(2,1)S(1)}, u32[]{:S(2)}, u32[]{:S(2)}) collective-permute-start(bf16[128,256]{1,0:T(8,128)(2,1)S(1)} %get-tuple-element.35), channel_id=1, source_target_pairs={{0,4},{1,5},{2,6},{3,7},{4,8},{5,9},{6,10},{7,11},{8,12},{9,13},{1... | collective-permute-start | bytes 196616 | tf_op jit(solution)/shard_map/ppermute | solution.py:363
  6.7 2.2 %collective-permute-start.3 = (bf16[128,256]{1,0:T(8,128)(2,1)S(1)}, bf16[128,256]{1,0:T(8,128)(2,1)S(1)}, u32[]{:S(2)}, u32[]{:S(2)}) collective-permute-start(bf16[128,256]{1,0:T(8,128)(2,1)S(1)} %get-tuple-element.36), channel_id=1, source_target_pairs={{0,12},{1,13},{2,14},{3,15},{4,0},{5,1},{6,2},{7,3},{8,4},{9,5},{1... | collective-permute-start | bytes 196616 | tf_op jit(solution)/shard_map/ppermute | solution.py:363
  9.0 1.3 %collective-permute-start.4 = (bf16[128,256]{1,0:T(8,128)(2,1)S(1)}, bf16[128,256]{1,0:T(8,128)(2,1)S(1)}, u32[]{:S(2)}, u32[]{:S(2)}) collective-permute-start(bf16[128,256]{1,0:T(8,128)(2,1)S(1)} %get-tuple-element.37), channel_id=1, source_target_pairs={{0,14},{1,15},{2,0},{3,1},{4,2},{5,3},{6,4},{7,5},{8,6},{9,7},{10,... | collective-permute-start | bytes 196616 | tf_op jit(solution)/shard_map/ppermute | solution.py:363
  10.3 4.1 %spread.1 = (bf16[2,256,8192]{2,1,0:T(8,128)(2,1)S(1)}, f32[2,256,8192]{2,1,0:T(8,128)S(1)}) custom-call(s32[2,8,128]{2,1,0:T(8,128)S(1)} %get-tuple-element.38.shifts_ref, f32[8,256]{1,0:T(8,128)S(1)} %get-tuple-element.39.table_ref, bf16[256,256]{1,0:T(8,128)(2,1)S(1)} %get-tuple-element.40.transform_ref, s32[2,8192]{1,0:T(2,128)S(1)} %get-tuple-element.41.row_ref, ...), custom_call_target="tpu_custom_call" | custom-call | flops 2147483648 | bytes 25165824 | tf_op jit(solution)/shard_map/spread/pallas_call | solution.py:366
  14.4 0.0 collective-permute-done.1.refs_1_
  14.4 0.0 collective-permute-done.2.refs_2_
  14.4 0.0 collective-permute-done.3.refs_3_
  14.4 0.0 collective-permute-done.4.refs_4_
  14.4 3.8 %degrid.1 = bf16[256,128]{1,0:T(8,128)(2,1)S(1)} custom-call(bf16[128,256]{1,0:T(8,128)(2,1)S(1)} %get-tuple-element.33.refs_0_, bf16[128,256]{1,0:T(8,128)(2,1)S(1)} %collective-permute-done.1.refs_1_, bf16[128,256]{1,0:T(8,128)(2,1)S(1)} %collective-permute-done.2.refs_2_, bf16[128,256]{1,0:T(8,128)(2,1)S(1)} %collective-permute-done.3.refs_3_, ...), custom_call_target="tpu_custom_call" | custom-call | tf_op jit(solution)/shard_map/degrid/pallas_call | solution.py:380
  18.2 11.0 %all_to_all.5 = bf16[16,16,128]{2,1,0:T(8,128)(2,1)S(1)} all-to-all(bf16[16,16,128]{2,1,0:T(8,128)(2,1)S(1)} %bitcast.4), channel_id=1, replica_groups=mesh['grp'=2,'row'=16] {'row'}, dimensions={0} | all-to-all | bytes 131072 | tf_op jit(solution)/shard_map/all_to_all | solution.py:392
  29.2 0.7 %place.1 = f32[2,32,512]{2,1,0:T(8,128)} custom-call(bf16[256,128]{1,0:T(8,128)(2,1)S(1)} %bitcast.5), custom_call_target="tpu_custom_call" | custom-call | tf_op jit(solution)/shard_map/place/pallas_call | solution.py:395
Async XLA Ops:
  0.0 2.2 %collective-permute-start = (bf16[2,16,32,128]{3,2,1,0:T(8,128)(2,1)}, bf16[2,16,32,128]{3,2,1,0:T(8,128)(2,1)S(1)}, u32[]{:S(2)}, u32[]{:S(2)}) collective-permute-start(bf16[2,16,32,128]{3,2,1,0:T(8,128)(2,1)} %refs_4_.1), channel_id=1, source_target_pairs={{0,1},{1,0},{2,3},{3,2},{4,5},{5,4},{6,7},{7,6},{8,9},{9,8},{10,11... | collective-permute-start | bytes 786440 | tf_op jit(solution)/shard_map/ppermute | solution.py:318
  2.6 11.8 %collective-permute-start.1 = (bf16[128,256]{1,0:T(8,128)(2,1)S(1)}, bf16[128,256]{1,0:T(8,128)(2,1)S(1)}, u32[]{:S(2)}, u32[]{:S(2)}) collective-permute-start(bf16[128,256]{1,0:T(8,128)(2,1)S(1)} %get-tuple-element.34), channel_id=1, source_target_pairs={{0,2},{1,3},{2,4},{3,5},{4,6},{5,7},{6,8},{7,9},{8,10},{9,11},{10,... | collective-permute-start | bytes 196616 | tf_op jit(solution)/shard_map/ppermute | solution.py:363
  5.1 9.2 %collective-permute-start.2 = (bf16[128,256]{1,0:T(8,128)(2,1)S(1)}, bf16[128,256]{1,0:T(8,128)(2,1)S(1)}, u32[]{:S(2)}, u32[]{:S(2)}) collective-permute-start(bf16[128,256]{1,0:T(8,128)(2,1)S(1)} %get-tuple-element.35), channel_id=1, source_target_pairs={{0,4},{1,5},{2,6},{3,7},{4,8},{5,9},{6,10},{7,11},{8,12},{9,13},{1... | collective-permute-start | bytes 196616 | tf_op jit(solution)/shard_map/ppermute | solution.py:363
  6.7 7.7 %collective-permute-start.3 = (bf16[128,256]{1,0:T(8,128)(2,1)S(1)}, bf16[128,256]{1,0:T(8,128)(2,1)S(1)}, u32[]{:S(2)}, u32[]{:S(2)}) collective-permute-start(bf16[128,256]{1,0:T(8,128)(2,1)S(1)} %get-tuple-element.36), channel_id=1, source_target_pairs={{0,12},{1,13},{2,14},{3,15},{4,0},{5,1},{6,2},{7,3},{8,4},{9,5},{1... | collective-permute-start | bytes 196616 | tf_op jit(solution)/shard_map/ppermute | solution.py:363
  9.0 5.4 %collective-permute-start.4 = (bf16[128,256]{1,0:T(8,128)(2,1)S(1)}, bf16[128,256]{1,0:T(8,128)(2,1)S(1)}, u32[]{:S(2)}, u32[]{:S(2)}) collective-permute-start(bf16[128,256]{1,0:T(8,128)(2,1)S(1)} %get-tuple-element.37), channel_id=1, source_target_pairs={{0,14},{1,15},{2,0},{3,1},{4,2},{5,3},{6,4},{7,5},{8,6},{9,7},{10,... | collective-permute-start | bytes 196616 | tf_op jit(solution)/shard_map/ppermute | solution.py:363

commit v4 on v3

--- a/solution.py
+++ b/solution.py
@@ -45,8 +45,17 @@
     return table
 
 
-SHIFTS = (1, 2, -2, -1)
+EXCHANGES = 4
 LATER = 6
+
+
+def reached(exchange, chip, chips):
+    return (
+        (chip + 2) % chips,
+        (((chip + 1) ^ 1) + chips - 1) % chips,
+        (chip + chips - 2) % chips,
+        chip ^ 1,
+    )[exchange]
 
 
 def facet_products(factors, rows_ref, outs, half_step, first_row):
@@ -142,8 +151,8 @@
             [jnp.where(diagonal, side, 0.0) for side in spread(part)]
             for part in (jnp.cos(angles), jnp.sin(angles))
         ]
-        for place, shift in enumerate((0,) + SHIFTS):
-            target = (chip + chips + shift) % chips
+        for place in range(1 + EXCHANGES):
+            target = chip if place == 0 else reached(place - 1, chip, chips)
             for sub in range(SUB_DEV):
                 subgrid = (target * 2 + core) * SUB_DEV + sub
                 slot = (base - start[subgrid]) & (total_rows - 1)
@@ -233,27 +242,29 @@
 def degrid_kernel(
     per_dest,
     own_ref,
-    below_ref,
     far_below_ref,
+    odd_edge_ref,
     far_above_ref,
-    above_ref,
+    even_edge_ref,
     row_spread,
     column_waves,
     out_ref,
     waves,
     gathered,
 ):
+    even = lax.axis_index("row") // 2 % 2 == 0
     wave = lax.broadcasted_iota(jnp.int32, (2 * KC, 2 * KC), 1)
     place = ((wave & (KC - 1)) >> 3) * 16 + (wave & 7) + jnp.where(wave < KC, 0, 8)
     turn = (lax.broadcasted_iota(jnp.int32, (2 * KC, 2 * KC), 0) == place).astype(jnp.float32).astype(jnp.bfloat16)
     for sub in range(SUB_DEV):
         rows = slice(sub * CHIP, sub * CHIP + CHIP)
+        odd_edge, even_edge = odd_edge_ref[rows, :], even_edge_ref[rows, :]
         summed = jnp.concatenate(
             [
                 own_ref[rows, :],
-                above_ref[rows, :],
+                jnp.where(even, even_edge, odd_edge),
                 far_below_ref[rows, :] + far_above_ref[rows, :],
-                below_ref[rows, :],
+                jnp.where(even, odd_edge, even_edge),
             ],
             axis=0,
         )
@@ -354,9 +365,9 @@
         name="other_facet_sums",
     )(other_rows, other_factors, shifts, *own_pieces)
     came = []
-    for shift, piece in zip(SHIFTS, pieces[1:]):
+    for exchange, piece in enumerate(pieces[1:]):
         pairs = [
-            (2 * chip + core, 2 * ((chip + shift) % chips) + core)
+            (2 * chip + core, 2 * reached(exchange, chip, chips) + core)
             for chip in range(chips)
             for core in range(2)
         ]

time: 30.1 us -> 29.1 us (0.967)
  blocking collectives: 11 us -> 9.86 us
    all_to_all x1, blocking collectives: 11 us -> 9.86 us  [local(): lax.all_to_all(results.reshape(devices, 4 * chunks, LANES), 'row', split_...]
  transfers between devices with their start and end apart: 5 -> 5, of which waited for: 0 -> 0; matrix products, arithmetic and copies ran while one was open for 0% -> 0% of each run, Pallas kernels for 19% -> 20%
where the time goes in v4:
time: 29.1 us; the launch traced here: 28.9 us
  Pallas kernels  10.6 us (36%)
  blocking collectives  9.86 us (34%)
  starting transfers between devices  8.37 us (29%)
    all_to_all x1, blocking collectives, local(): lax.all_to_all(results.reshape(devices, 4 * chunks, LANES), 'row', split_...  9.86 us
    ppermute x4, starting transfers between devices, local(): came.append(lax.ppermute(piece, 'row', pairs))  7.91 us
    pallas_call x1, Pallas kernels, local(): pl.pallas_call(spread_kernel, out_shape=[jax.ShapeDtypeStruct(spread_shap...  4.06 us
    pallas_call x1, Pallas kernels, local(): pl.pallas_call(lambda *refs: degrid_kernel(per_dest, *refs), out_shape=ja...  3.78 us
    pallas_call x1, Pallas kernels, local(): pl.pallas_call(lambda *refs: own_facet_kernel(devices, *refs), out_shape=...  1.75 us
    pallas_call x1, Pallas kernels, local(): pl.pallas_call(lambda *refs: place_kernel(devices, chunks, *refs), out_sh...  0.69 us
  transfers between devices with their start and end apart: 5, of which 0 were waited for; matrix products, arithmetic and copies ran while one was open for 0% of the time, Pallas kernels for 20%

profile of v4, /device:TPU:0, one launch (start us, length us, event | category | flops | bytes accessed | tf_op | source)
XLA Modules:
  0.0 28.9 jit_solution(4637520814686989646)
XLA Ops:
  0.0 0.5 %collective-permute-start = (bf16[2,16,32,128]{3,2,1,0:T(8,128)(2,1)}, bf16[2,16,32,128]{3,2,1,0:T(8,128)(2,1)S(1)}, u32[]{:S(2)}, u32[]{:S(2)}) collective-permute-start(bf16[2,16,32,128]{3,2,1,0:T(8,128)(2,1)} %refs_4_.1), channel_id=1, source_target_pairs={{0,1},{1,0},{2,3},{3,2},{4,5},{5,4},{6,7},{7,6},{8,9},{9,8},{10,11... | collective-permute-start | bytes 786440 | tf_op jit(solution)/shard_map/ppermute | solution.py:329
  0.5 1.8 %own_facet_sums.1 = (bf16[64,256]{1,0:T(8,128)(2,1)S(1)}, bf16[64,256]{1,0:T(8,128)(2,1)S(1)}, bf16[64,256]{1,0:T(8,128)(2,1)S(1)}, bf16[64,256]{1,0:T(8,128)(2,...) custom-call(s32[32]{0:T(128)} %refs_0_.1, ...), custom_call_target="tpu_custom_call" | custom-call | tf_op jit(solution)/shard_map/own_facet_sums/pallas_call | solution.py:333
  2.2 0.0 collective-permute-done.rows_ref
  2.2 0.3 %other_facet_sums.1 = (bf16[128,256]{1,0:T(8,128)(2,1)S(1)}, bf16[128,256]{1,0:T(8,128)(2,1)S(1)}, bf16[128,256]{1,0:T(8,128)(2,1)S(1)}, bf16[128,256]{1,0:T(8,1...) custom-call(bf16[2,16,32,128]{3,2,1,0:T(8,128)(2,1)S(1)} %collective-permute-done.rows_ref, ...), custom_call_target="tpu_custom_call" | custom-call | tf_op jit(solution)/shard_map/other_facet_sums/pallas_call | solution.py:358
  2.6 2.6 %collective-permute-start.1 = (bf16[128,256]{1,0:T(8,128)(2,1)S(1)}, bf16[128,256]{1,0:T(8,128)(2,1)S(1)}, u32[]{:S(2)}, u32[]{:S(2)}) collective-permute-start(bf16[128,256]{1,0:T(8,128)(2,1)S(1)} %get-tuple-element.34), channel_id=1, source_target_pairs={{0,4},{1,5},{2,6},{3,7},{4,8},{5,9},{6,10},{7,11},{8,12},{9,13},{1... | collective-permute-start | bytes 196616 | tf_op jit(solution)/shard_map/ppermute | solution.py:374
  5.2 3.2 %collective-permute-start.2 = (bf16[128,256]{1,0:T(8,128)(2,1)S(1)}, bf16[128,256]{1,0:T(8,128)(2,1)S(1)}, u32[]{:S(2)}, u32[]{:S(2)}) collective-permute-start(bf16[128,256]{1,0:T(8,128)(2,1)S(1)} %get-tuple-element.35), channel_id=1, source_target_pairs={{0,14},{1,15},{2,4},{3,5},{4,2},{5,3},{6,8},{7,9},{8,6},{9,7},{10,... | collective-permute-start | bytes 196616 | tf_op jit(solution)/shard_map/ppermute | solution.py:374
  8.4 1.8 %collective-permute-start.3 = (bf16[128,256]{1,0:T(8,128)(2,1)S(1)}, bf16[128,256]{1,0:T(8,128)(2,1)S(1)}, u32[]{:S(2)}, u32[]{:S(2)}) collective-permute-start(bf16[128,256]{1,0:T(8,128)(2,1)S(1)} %get-tuple-element.36), channel_id=1, source_target_pairs={{0,12},{1,13},{2,14},{3,15},{4,0},{5,1},{6,2},{7,3},{8,4},{9,5},{1... | collective-permute-start | bytes 196616 | tf_op jit(solution)/shard_map/ppermute | solution.py:374
  10.2 0.3 collective-permute-start.4
  10.5 4.1 %spread.1 = (bf16[2,256,8192]{2,1,0:T(8,128)(2,1)S(1)}, f32[2,256,8192]{2,1,0:T(8,128)S(1)}) custom-call(s32[2,8,128]{2,1,0:T(8,128)S(1)} %get-tuple-element.38.shifts_ref, f32[8,256]{1,0:T(8,128)S(1)} %get-tuple-element.39.table_ref, bf16[256,256]{1,0:T(8,128)(2,1)S(1)} %get-tuple-element.40.transform_ref, s32[2,8192]{1,0:T(2,128)S(1)} %get-tuple-element.41.row_ref, ...), custom_call_target="tpu_custom_call" | custom-call | flops 2147483648 | bytes 25165824 | tf_op jit(solution)/shard_map/spread/pallas_call | solution.py:377
  14.6 0.0 collective-permute-done.1.refs_1_
  14.6 0.0 collective-permute-done.2.refs_2_
  14.6 0.0 collective-permute-done.3.refs_3_
  14.6 0.0 collective-permute-done.4.refs_4_
  14.6 3.8 %degrid.1 = bf16[256,128]{1,0:T(8,128)(2,1)S(1)} custom-call(bf16[128,256]{1,0:T(8,128)(2,1)S(1)} %get-tuple-element.33.refs_0_, bf16[128,256]{1,0:T(8,128)(2,1)S(1)} %collective-permute-done.1.refs_1_, bf16[128,256]{1,0:T(8,128)(2,1)S(1)} %collective-permute-done.2.refs_2_, bf16[128,256]{1,0:T(8,128)(2,1)S(1)} %collective-permute-done.3.refs_3_, ...), custom_call_target="tpu_custom_call" | custom-call | tf_op jit(solution)/shard_map/degrid/pallas_call | solution.py:391
  18.4 9.9 %all_to_all.5 = bf16[16,16,128]{2,1,0:T(8,128)(2,1)S(1)} all-to-all(bf16[16,16,128]{2,1,0:T(8,128)(2,1)S(1)} %bitcast.4), channel_id=1, replica_groups=mesh['grp'=2,'row'=16] {'row'}, dimensions={0} | all-to-all | bytes 131072 | tf_op jit(solution)/shard_map/all_to_all | solution.py:403
  28.3 0.7 %place.1 = f32[2,32,512]{2,1,0:T(8,128)} custom-call(bf16[256,128]{1,0:T(8,128)(2,1)S(1)} %bitcast.5), custom_call_target="tpu_custom_call" | custom-call | tf_op jit(solution)/shard_map/place/pallas_call | solution.py:406
Async XLA Ops:
  0.0 2.2 %collective-permute-start = (bf16[2,16,32,128]{3,2,1,0:T(8,128)(2,1)}, bf16[2,16,32,128]{3,2,1,0:T(8,128)(2,1)S(1)}, u32[]{:S(2)}, u32[]{:S(2)}) collective-permute-start(bf16[2,16,32,128]{3,2,1,0:T(8,128)(2,1)} %refs_4_.1), channel_id=1, source_target_pairs={{0,1},{1,0},{2,3},{3,2},{4,5},{5,4},{6,7},{7,6},{8,9},{9,8},{10,11... | collective-permute-start | bytes 786440 | tf_op jit(solution)/shard_map/ppermute | solution.py:329
  2.6 12.0 %collective-permute-start.1 = (bf16[128,256]{1,0:T(8,128)(2,1)S(1)}, bf16[128,256]{1,0:T(8,128)(2,1)S(1)}, u32[]{:S(2)}, u32[]{:S(2)}) collective-permute-start(bf16[128,256]{1,0:T(8,128)(2,1)S(1)} %get-tuple-element.34), channel_id=1, source_target_pairs={{0,4},{1,5},{2,6},{3,7},{4,8},{5,9},{6,10},{7,11},{8,12},{9,13},{1... | collective-permute-start | bytes 196616 | tf_op jit(solution)/shard_map/ppermute | solution.py:374
  5.2 9.4 %collective-permute-start.2 = (bf16[128,256]{1,0:T(8,128)(2,1)S(1)}, bf16[128,256]{1,0:T(8,128)(2,1)S(1)}, u32[]{:S(2)}, u32[]{:S(2)}) collective-permute-start(bf16[128,256]{1,0:T(8,128)(2,1)S(1)} %get-tuple-element.35), channel_id=1, source_target_pairs={{0,14},{1,15},{2,4},{3,5},{4,2},{5,3},{6,8},{7,9},{8,6},{9,7},{10,... | collective-permute-start | bytes 196616 | tf_op jit(solution)/shard_map/ppermute | solution.py:374
  8.4 6.2 %collective-permute-start.3 = (bf16[128,256]{1,0:T(8,128)(2,1)S(1)}, bf16[128,256]{1,0:T(8,128)(2,1)S(1)}, u32[]{:S(2)}, u32[]{:S(2)}) collective-permute-start(bf16[128,256]{1,0:T(8,128)(2,1)S(1)} %get-tuple-element.36), channel_id=1, source_target_pairs={{0,12},{1,13},{2,14},{3,15},{4,0},{5,1},{6,2},{7,3},{8,4},{9,5},{1... | collective-permute-start | bytes 196616 | tf_op jit(solution)/shard_map/ppermute | solution.py:374
  10.2 4.4 %collective-permute-start.4 = (bf16[128,256]{1,0:T(8,128)(2,1)S(1)}, bf16[128,256]{1,0:T(8,128)(2,1)S(1)}, u32[]{:S(2)}, u32[]{:S(2)}) collective-permute-start(bf16[128,256]{1,0:T(8,128)(2,1)S(1)} %get-tuple-element.37), channel_id=1, source_target_pairs={{0,2},{1,3},{2,0},{3,1},{4,6},{5,7},{6,4},{7,5},{8,10},{9,11},{10,... | collective-permute-start | bytes 196616 | tf_op jit(solution)/shard_map/ppermute | solution.py:374

commit v5 on v4

--- a/solution.py
+++ b/solution.py
@@ -154,7 +154,7 @@
         for place in range(1 + EXCHANGES):
             target = chip if place == 0 else reached(place - 1, chip, chips)
             for sub in range(SUB_DEV):
-                subgrid = (target * 2 + core) * SUB_DEV + sub
+                subgrid = (target * 2 + (core if place == 0 else 1 - core)) * SUB_DEV + sub
                 slot = (base - start[subgrid]) & (total_rows - 1)
                 slot = jnp.where(slot > total_rows - R_DEV, slot - total_rows, slot)
                 slot = jnp.minimum(slot, SUB)
@@ -367,7 +367,7 @@
     came = []
     for exchange, piece in enumerate(pieces[1:]):
         pairs = [
-            (2 * chip + core, 2 * reached(exchange, chip, chips) + core)
+            (2 * chip + core, 2 * reached(exchange, chip, chips) + 1 - core)
             for chip in range(chips)
             for core in range(2)
         ]

time: 29.1 us -> 28.7 us (0.986)
  starting transfers between devices: 8.37 us -> 7.92 us
    ppermute x4, starting transfers between devices: 7.91 us -> 7.47 us  [local(): came.append(lax.ppermute(piece, 'row', pairs))]
  transfers between devices with their start and end apart: 5 -> 5, of which waited for: 0 -> 1; matrix products, arithmetic and copies ran while one was open for 0% -> 0% of each run, Pallas kernels for 20% -> 20%
where the time goes in v5:
time: 28.7 us; the launch traced here: 28.5 us
  Pallas kernels  10.6 us (37%)
  blocking collectives  9.77 us (34%)
  starting transfers between devices  7.92 us (28%)
    all_to_all x1, blocking collectives, local(): lax.all_to_all(results.reshape(devices, 4 * chunks, LANES), 'row', split_...  9.77 us
    ppermute x4, starting transfers between devices, local(): came.append(lax.ppermute(piece, 'row', pairs))  7.47 us
    pallas_call x1, Pallas kernels, local(): pl.pallas_call(spread_kernel, out_shape=[jax.ShapeDtypeStruct(spread_shap...  4.07 us
    pallas_call x1, Pallas kernels, local(): pl.pallas_call(lambda *refs: degrid_kernel(per_dest, *refs), out_shape=ja...  3.77 us
    pallas_call x1, Pallas kernels, local(): pl.pallas_call(lambda *refs: own_facet_kernel(devices, *refs), out_shape=...  1.75 us
    pallas_call x1, Pallas kernels, local(): pl.pallas_call(lambda *refs: place_kernel(devices, chunks, *refs), out_sh...  0.69 us
  transfers between devices with their start and end apart: 5, of which 1 were waited for; matrix products, arithmetic and copies ran while one was open for 0% of the time, Pallas kernels for 20%

profile of v5, /device:TPU:0, one launch (start us, length us, event | category | flops | bytes accessed | tf_op | source)
XLA Modules:
  0.0 28.5 jit_solution(2792722604806299500)
XLA Ops:
  0.0 0.5 %collective-permute-start = (bf16[2,16,32,128]{3,2,1,0:T(8,128)(2,1)}, bf16[2,16,32,128]{3,2,1,0:T(8,128)(2,1)S(1)}, u32[]{:S(2)}, u32[]{:S(2)}) collective-permute-start(bf16[2,16,32,128]{3,2,1,0:T(8,128)(2,1)} %refs_4_.1), channel_id=1, source_target_pairs={{0,1},{1,0},{2,3},{3,2},{4,5},{5,4},{6,7},{7,6},{8,9},{9,8},{10,11... | collective-permute-start | bytes 786440 | tf_op jit(solution)/shard_map/ppermute | solution.py:329
  0.5 1.8 %own_facet_sums.1 = (bf16[64,256]{1,0:T(8,128)(2,1)S(1)}, bf16[64,256]{1,0:T(8,128)(2,1)S(1)}, bf16[64,256]{1,0:T(8,128)(2,1)S(1)}, bf16[64,256]{1,0:T(8,128)(2,...) custom-call(s32[32]{0:T(128)} %refs_0_.1, ...), custom_call_target="tpu_custom_call" | custom-call | tf_op jit(solution)/shard_map/own_facet_sums/pallas_call | solution.py:333
  2.2 0.0 collective-permute-done.rows_ref
  2.2 0.3 %other_facet_sums.1 = (bf16[128,256]{1,0:T(8,128)(2,1)S(1)}, bf16[128,256]{1,0:T(8,128)(2,1)S(1)}, bf16[128,256]{1,0:T(8,128)(2,1)S(1)}, bf16[128,256]{1,0:T(8,1...) custom-call(bf16[2,16,32,128]{3,2,1,0:T(8,128)(2,1)S(1)} %collective-permute-done.rows_ref, ...), custom_call_target="tpu_custom_call" | custom-call | tf_op jit(solution)/shard_map/other_facet_sums/pallas_call | solution.py:358
  2.6 2.7 %collective-permute-start.1 = (bf16[128,256]{1,0:T(8,128)(2,1)S(1)}, bf16[128,256]{1,0:T(8,128)(2,1)S(1)}, u32[]{:S(2)}, u32[]{:S(2)}) collective-permute-start(bf16[128,256]{1,0:T(8,128)(2,1)S(1)} %get-tuple-element.34), channel_id=1, source_target_pairs={{0,5},{1,4},{2,7},{3,6},{4,9},{5,8},{6,11},{7,10},{8,13},{9,12},{1... | collective-permute-start | bytes 196616 | tf_op jit(solution)/shard_map/ppermute | solution.py:374
  5.3 3.1 %collective-permute-start.2 = (bf16[128,256]{1,0:T(8,128)(2,1)S(1)}, bf16[128,256]{1,0:T(8,128)(2,1)S(1)}, u32[]{:S(2)}, u32[]{:S(2)}) collective-permute-start(bf16[128,256]{1,0:T(8,128)(2,1)S(1)} %get-tuple-element.35), channel_id=1, source_target_pairs={{0,15},{1,14},{2,5},{3,4},{4,3},{5,2},{6,9},{7,8},{8,7},{9,6},{10,... | collective-permute-start | bytes 196616 | tf_op jit(solution)/shard_map/ppermute | solution.py:374
  8.4 1.7 %collective-permute-start.3 = (bf16[128,256]{1,0:T(8,128)(2,1)S(1)}, bf16[128,256]{1,0:T(8,128)(2,1)S(1)}, u32[]{:S(2)}, u32[]{:S(2)}) collective-permute-start(bf16[128,256]{1,0:T(8,128)(2,1)S(1)} %get-tuple-element.36), channel_id=1, source_target_pairs={{0,13},{1,12},{2,15},{3,14},{4,1},{5,0},{6,3},{7,2},{8,5},{9,4},{1... | collective-permute-start | bytes 196616 | tf_op jit(solution)/shard_map/ppermute | solution.py:374
  10.0 0.0 collective-permute-start.4
  10.0 4.1 %spread.1 = (bf16[2,256,8192]{2,1,0:T(8,128)(2,1)S(1)}, f32[2,256,8192]{2,1,0:T(8,128)S(1)}) custom-call(s32[2,8,128]{2,1,0:T(8,128)S(1)} %get-tuple-element.38.shifts_ref, f32[8,256]{1,0:T(8,128)S(1)} %get-tuple-element.39.table_ref, bf16[256,256]{1,0:T(8,128)(2,1)S(1)} %get-tuple-element.40.transform_ref, s32[2,8192]{1,0:T(2,128)S(1)} %get-tuple-element.41.row_ref, ...), custom_call_target="tpu_custom_call" | custom-call | flops 2147483648 | bytes 25165824 | tf_op jit(solution)/shard_map/spread/pallas_call | solution.py:377
  14.1 0.0 collective-permute-done.1.refs_1_
  14.1 0.0 collective-permute-done.2.refs_2_
  14.1 0.0 collective-permute-done.3.refs_3_
  14.2 0.1 collective-permute-done.4.refs_4_
  14.3 3.8 %degrid.1 = bf16[256,128]{1,0:T(8,128)(2,1)S(1)} custom-call(bf16[128,256]{1,0:T(8,128)(2,1)S(1)} %get-tuple-element.33.refs_0_, bf16[128,256]{1,0:T(8,128)(2,1)S(1)} %collective-permute-done.1.refs_1_, bf16[128,256]{1,0:T(8,128)(2,1)S(1)} %collective-permute-done.2.refs_2_, bf16[128,256]{1,0:T(8,128)(2,1)S(1)} %collective-permute-done.3.refs_3_, ...), custom_call_target="tpu_custom_call" | custom-call | tf_op jit(solution)/shard_map/degrid/pallas_call | solution.py:391
  18.0 9.8 %all_to_all.5 = bf16[16,16,128]{2,1,0:T(8,128)(2,1)S(1)} all-to-all(bf16[16,16,128]{2,1,0:T(8,128)(2,1)S(1)} %bitcast.4), channel_id=1, replica_groups=mesh['grp'=2,'row'=16] {'row'}, dimensions={0} | all-to-all | bytes 131072 | tf_op jit(solution)/shard_map/all_to_all | solution.py:403
  27.8 0.7 %place.1 = f32[2,32,512]{2,1,0:T(8,128)} custom-call(bf16[256,128]{1,0:T(8,128)(2,1)S(1)} %bitcast.5), custom_call_target="tpu_custom_call" | custom-call | tf_op jit(solution)/shard_map/place/pallas_call | solution.py:406
Async XLA Ops:
  0.0 2.2 %collective-permute-start = (bf16[2,16,32,128]{3,2,1,0:T(8,128)(2,1)}, bf16[2,16,32,128]{3,2,1,0:T(8,128)(2,1)S(1)}, u32[]{:S(2)}, u32[]{:S(2)}) collective-permute-start(bf16[2,16,32,128]{3,2,1,0:T(8,128)(2,1)} %refs_4_.1), channel_id=1, source_target_pairs={{0,1},{1,0},{2,3},{3,2},{4,5},{5,4},{6,7},{7,6},{8,9},{9,8},{10,11... | collective-permute-start | bytes 786440 | tf_op jit(solution)/shard_map/ppermute | solution.py:329
  2.6 11.6 %collective-permute-start.1 = (bf16[128,256]{1,0:T(8,128)(2,1)S(1)}, bf16[128,256]{1,0:T(8,128)(2,1)S(1)}, u32[]{:S(2)}, u32[]{:S(2)}) collective-permute-start(bf16[128,256]{1,0:T(8,128)(2,1)S(1)} %get-tuple-element.34), channel_id=1, source_target_pairs={{0,5},{1,4},{2,7},{3,6},{4,9},{5,8},{6,11},{7,10},{8,13},{9,12},{1... | collective-permute-start | bytes 196616 | tf_op jit(solution)/shard_map/ppermute | solution.py:374
  5.3 8.8 %collective-permute-start.2 = (bf16[128,256]{1,0:T(8,128)(2,1)S(1)}, bf16[128,256]{1,0:T(8,128)(2,1)S(1)}, u32[]{:S(2)}, u32[]{:S(2)}) collective-permute-start(bf16[128,256]{1,0:T(8,128)(2,1)S(1)} %get-tuple-element.35), channel_id=1, source_target_pairs={{0,15},{1,14},{2,5},{3,4},{4,3},{5,2},{6,9},{7,8},{8,7},{9,6},{10,... | collective-permute-start | bytes 196616 | tf_op jit(solution)/shard_map/ppermute | solution.py:374
  8.4 5.8 %collective-permute-start.3 = (bf16[128,256]{1,0:T(8,128)(2,1)S(1)}, bf16[128,256]{1,0:T(8,128)(2,1)S(1)}, u32[]{:S(2)}, u32[]{:S(2)}) collective-permute-start(bf16[128,256]{1,0:T(8,128)(2,1)S(1)} %get-tuple-element.36), channel_id=1, source_target_pairs={{0,13},{1,12},{2,15},{3,14},{4,1},{5,0},{6,3},{7,2},{8,5},{9,4},{1... | collective-permute-start | bytes 196616 | tf_op jit(solution)/shard_map/ppermute | solution.py:374
  10.0 4.2 %collective-permute-start.4 = (bf16[128,256]{1,0:T(8,128)(2,1)S(1)}, bf16[128,256]{1,0:T(8,128)(2,1)S(1)}, u32[]{:S(2)}, u32[]{:S(2)}) collective-permute-start(bf16[128,256]{1,0:T(8,128)(2,1)S(1)} %get-tuple-element.37), channel_id=1, source_target_pairs={{0,3},{1,2},{2,1},{3,0},{4,7},{5,6},{6,5},{7,4},{8,11},{9,10},{10,... | collective-permute-start | bytes 196616 | tf_op jit(solution)/shard_map/ppermute | solution.py:374

commit v6 on v5

--- a/solution.py
+++ b/solution.py
@@ -18,9 +18,9 @@
 CHIP = 2 * R_DEV
 LANES = 128
 BLOCK = 1024
-UNROLL = 4
+UNROLL = 8
 PART = 512
-PART_UNROLL = 8
+PART_UNROLL = 16
 
 TWO_PI = 2.0 * math.pi
 

time: 28.7 us -> 28.2 us (0.983)
  Pallas kernels: 10.6 us -> 10.1 us
    pallas_call x1, Pallas kernels: 3.77 us -> 3.35 us  [local(): pl.pallas_call(lambda *refs: degrid_kernel(per_dest, *refs), out_shape=ja...]
  transfers between devices with their start and end apart: 5 -> 5, of which waited for: 1 -> 1; matrix products, arithmetic and copies ran while one was open for 0% -> 0% of each run, Pallas kernels for 20% -> 21%
where the time goes in v6:
time: 28.2 us; the launch traced here: 28 us
  Pallas kernels  10.1 us (36%)
  blocking collectives  9.68 us (34%)
  starting transfers between devices  7.92 us (28%)
    all_to_all x1, blocking collectives, local(): lax.all_to_all(results.reshape(devices, 4 * chunks, LANES), 'row', split_...  9.68 us
    ppermute x4, starting transfers between devices, local(): came.append(lax.ppermute(piece, 'row', pairs))  7.47 us
    pallas_call x1, Pallas kernels, local(): pl.pallas_call(spread_kernel, out_shape=[jax.ShapeDtypeStruct(spread_shap...  4 us
    pallas_call x1, Pallas kernels, local(): pl.pallas_call(lambda *refs: degrid_kernel(per_dest, *refs), out_shape=ja...  3.35 us
    pallas_call x1, Pallas kernels, local(): pl.pallas_call(lambda *refs: own_facet_kernel(devices, *refs), out_shape=...  1.76 us
    pallas_call x1, Pallas kernels, local(): pl.pallas_call(lambda *refs: place_kernel(devices, chunks, *refs), out_sh...  0.69 us
  transfers between devices with their start and end apart: 5, of which 1 were waited for; matrix products, arithmetic and copies ran while one was open for 0% of the time, Pallas kernels for 21%

profile of v6, /device:TPU:0, one launch (start us, length us, event | category | flops | bytes accessed | tf_op | source)
XLA Modules:
  0.0 28.0 jit_solution(7969308141208135558)
XLA Ops:
  0.0 0.5 %collective-permute-start = (bf16[2,16,32,128]{3,2,1,0:T(8,128)(2,1)}, bf16[2,16,32,128]{3,2,1,0:T(8,128)(2,1)S(1)}, u32[]{:S(2)}, u32[]{:S(2)}) collective-permute-start(bf16[2,16,32,128]{3,2,1,0:T(8,128)(2,1)} %refs_4_.1), channel_id=1, source_target_pairs={{0,1},{1,0},{2,3},{3,2},{4,5},{5,4},{6,7},{7,6},{8,9},{9,8},{10,11... | collective-permute-start | bytes 786440 | tf_op jit(solution)/shard_map/ppermute | solution.py:329
  0.5 1.8 %own_facet_sums.1 = (bf16[64,256]{1,0:T(8,128)(2,1)S(1)}, bf16[64,256]{1,0:T(8,128)(2,1)S(1)}, bf16[64,256]{1,0:T(8,128)(2,1)S(1)}, bf16[64,256]{1,0:T(8,128)(2,...) custom-call(s32[32]{0:T(128)} %refs_0_.1, ...), custom_call_target="tpu_custom_call" | custom-call | tf_op jit(solution)/shard_map/own_facet_sums/pallas_call | solution.py:333
  2.2 0.0 collective-permute-done.rows_ref
  2.2 0.3 %other_facet_sums.1 = (bf16[128,256]{1,0:T(8,128)(2,1)S(1)}, bf16[128,256]{1,0:T(8,128)(2,1)S(1)}, bf16[128,256]{1,0:T(8,128)(2,1)S(1)}, bf16[128,256]{1,0:T(8,1...) custom-call(bf16[2,16,32,128]{3,2,1,0:T(8,128)(2,1)S(1)} %collective-permute-done.rows_ref, ...), custom_call_target="tpu_custom_call" | custom-call | tf_op jit(solution)/shard_map/other_facet_sums/pallas_call | solution.py:358
  2.6 2.7 %collective-permute-start.1 = (bf16[128,256]{1,0:T(8,128)(2,1)S(1)}, bf16[128,256]{1,0:T(8,128)(2,1)S(1)}, u32[]{:S(2)}, u32[]{:S(2)}) collective-permute-start(bf16[128,256]{1,0:T(8,128)(2,1)S(1)} %get-tuple-element.34), channel_id=1, source_target_pairs={{0,5},{1,4},{2,7},{3,6},{4,9},{5,8},{6,11},{7,10},{8,13},{9,12},{1... | collective-permute-start | bytes 196616 | tf_op jit(solution)/shard_map/ppermute | solution.py:374
  5.3 3.1 %collective-permute-start.2 = (bf16[128,256]{1,0:T(8,128)(2,1)S(1)}, bf16[128,256]{1,0:T(8,128)(2,1)S(1)}, u32[]{:S(2)}, u32[]{:S(2)}) collective-permute-start(bf16[128,256]{1,0:T(8,128)(2,1)S(1)} %get-tuple-element.35), channel_id=1, source_target_pairs={{0,15},{1,14},{2,5},{3,4},{4,3},{5,2},{6,9},{7,8},{8,7},{9,6},{10,... | collective-permute-start | bytes 196616 | tf_op jit(solution)/shard_map/ppermute | solution.py:374
  8.4 1.7 %collective-permute-start.3 = (bf16[128,256]{1,0:T(8,128)(2,1)S(1)}, bf16[128,256]{1,0:T(8,128)(2,1)S(1)}, u32[]{:S(2)}, u32[]{:S(2)}) collective-permute-start(bf16[128,256]{1,0:T(8,128)(2,1)S(1)} %get-tuple-element.36), channel_id=1, source_target_pairs={{0,13},{1,12},{2,15},{3,14},{4,1},{5,0},{6,3},{7,2},{8,5},{9,4},{1... | collective-permute-start | bytes 196616 | tf_op jit(solution)/shard_map/ppermute | solution.py:374
  10.0 0.0 collective-permute-start.4
  10.0 4.0 %spread.1 = (bf16[2,256,8192]{2,1,0:T(8,128)(2,1)S(1)}, f32[2,256,8192]{2,1,0:T(8,128)S(1)}) custom-call(s32[2,8,128]{2,1,0:T(8,128)S(1)} %get-tuple-element.38.shifts_ref, f32[8,256]{1,0:T(8,128)S(1)} %get-tuple-element.39.table_ref, bf16[256,256]{1,0:T(8,128)(2,1)S(1)} %get-tuple-element.40.transform_ref, s32[2,8192]{1,0:T(2,128)S(1)} %get-tuple-element.41.row_ref, ...), custom_call_target="tpu_custom_call" | custom-call | flops 2147483648 | bytes 25165824 | tf_op jit(solution)/shard_map/spread/pallas_call | solution.py:377
  14.1 0.0 collective-permute-done.1.refs_1_
  14.1 0.0 collective-permute-done.2.refs_2_
  14.1 0.0 collective-permute-done.3.refs_3_
  14.1 0.2 collective-permute-done.4.refs_4_
  14.3 3.4 %degrid.1 = bf16[256,128]{1,0:T(8,128)(2,1)S(1)} custom-call(bf16[128,256]{1,0:T(8,128)(2,1)S(1)} %get-tuple-element.33.refs_0_, bf16[128,256]{1,0:T(8,128)(2,1)S(1)} %collective-permute-done.1.refs_1_, bf16[128,256]{1,0:T(8,128)(2,1)S(1)} %collective-permute-done.2.refs_2_, bf16[128,256]{1,0:T(8,128)(2,1)S(1)} %collective-permute-done.3.refs_3_, ...), custom_call_target="tpu_custom_call" | custom-call | tf_op jit(solution)/shard_map/degrid/pallas_call | solution.py:391
  17.6 9.7 %all_to_all.5 = bf16[16,16,128]{2,1,0:T(8,128)(2,1)S(1)} all-to-all(bf16[16,16,128]{2,1,0:T(8,128)(2,1)S(1)} %bitcast.4), channel_id=1, replica_groups=mesh['grp'=2,'row'=16] {'row'}, dimensions={0} | all-to-all | bytes 131072 | tf_op jit(solution)/shard_map/all_to_all | solution.py:403
  27.3 0.7 %place.1 = f32[2,32,512]{2,1,0:T(8,128)} custom-call(bf16[256,128]{1,0:T(8,128)(2,1)S(1)} %bitcast.5), custom_call_target="tpu_custom_call" | custom-call | tf_op jit(solution)/shard_map/place/pallas_call | solution.py:406
Async XLA Ops:
  0.0 2.2 %collective-permute-start = (bf16[2,16,32,128]{3,2,1,0:T(8,128)(2,1)}, bf16[2,16,32,128]{3,2,1,0:T(8,128)(2,1)S(1)}, u32[]{:S(2)}, u32[]{:S(2)}) collective-permute-start(bf16[2,16,32,128]{3,2,1,0:T(8,128)(2,1)} %refs_4_.1), channel_id=1, source_target_pairs={{0,1},{1,0},{2,3},{3,2},{4,5},{5,4},{6,7},{7,6},{8,9},{9,8},{10,11... | collective-permute-start | bytes 786440 | tf_op jit(solution)/shard_map/ppermute | solution.py:329
  2.6 11.5 %collective-permute-start.1 = (bf16[128,256]{1,0:T(8,128)(2,1)S(1)}, bf16[128,256]{1,0:T(8,128)(2,1)S(1)}, u32[]{:S(2)}, u32[]{:S(2)}) collective-permute-start(bf16[128,256]{1,0:T(8,128)(2,1)S(1)} %get-tuple-element.34), channel_id=1, source_target_pairs={{0,5},{1,4},{2,7},{3,6},{4,9},{5,8},{6,11},{7,10},{8,13},{9,12},{1... | collective-permute-start | bytes 196616 | tf_op jit(solution)/shard_map/ppermute | solution.py:374
  5.3 8.8 %collective-permute-start.2 = (bf16[128,256]{1,0:T(8,128)(2,1)S(1)}, bf16[128,256]{1,0:T(8,128)(2,1)S(1)}, u32[]{:S(2)}, u32[]{:S(2)}) collective-permute-start(bf16[128,256]{1,0:T(8,128)(2,1)S(1)} %get-tuple-element.35), channel_id=1, source_target_pairs={{0,15},{1,14},{2,5},{3,4},{4,3},{5,2},{6,9},{7,8},{8,7},{9,6},{10,... | collective-permute-start | bytes 196616 | tf_op jit(solution)/shard_map/ppermute | solution.py:374
  8.4 5.7 %collective-permute-start.3 = (bf16[128,256]{1,0:T(8,128)(2,1)S(1)}, bf16[128,256]{1,0:T(8,128)(2,1)S(1)}, u32[]{:S(2)}, u32[]{:S(2)}) collective-permute-start(bf16[128,256]{1,0:T(8,128)(2,1)S(1)} %get-tuple-element.36), channel_id=1, source_target_pairs={{0,13},{1,12},{2,15},{3,14},{4,1},{5,0},{6,3},{7,2},{8,5},{9,4},{1... | collective-permute-start | bytes 196616 | tf_op jit(solution)/shard_map/ppermute | solution.py:374
  10.0 4.2 %collective-permute-start.4 = (bf16[128,256]{1,0:T(8,128)(2,1)S(1)}, bf16[128,256]{1,0:T(8,128)(2,1)S(1)}, u32[]{:S(2)}, u32[]{:S(2)}) collective-permute-start(bf16[128,256]{1,0:T(8,128)(2,1)S(1)} %get-tuple-element.37), channel_id=1, source_target_pairs={{0,3},{1,2},{2,1},{3,0},{4,7},{5,6},{6,5},{7,4},{8,11},{9,10},{10,... | collective-permute-start | bytes 196616 | tf_op jit(solution)/shard_map/ppermute | solution.py:374

commit v7 on v6

--- a/solution.py
+++ b/solution.py
@@ -171,8 +171,9 @@
                             here = slice((place * SUB_DEV + sub) * 16, (place * SUB_DEV + sub) * 16 + 16)
                             factors[group, 2 * kind, here, lanes] = high[rows]
                             factors[group, 2 * kind + 1, here, lanes] = low[rows]
-    copies[4].wait()
-    facet_products(lambda group, kind: own_factors[group, kind], rows_ref, outs, R_DEV, 0)
+        if held == 0:
+            copies[4].wait()
+            facet_products(lambda group, kind: own_factors[group, kind], rows_ref, outs, R_DEV, 0)
     for copy in copies[5:]:
         copy.wait()
 

time: 28.2 us -> 28 us (level)
  transfers between devices with their start and end apart: 5 -> 5, of which waited for: 1 -> 0; matrix products, arithmetic and copies ran while one was open for 0% -> 0% of each run, Pallas kernels for 21% -> 20%
where the time goes in v7:
time: 28 us; the launch traced here: 27.8 us
  Pallas kernels  9.94 us (36%)
  blocking collectives  9.81 us (35%)
  starting transfers between devices  7.98 us (28%)
    all_to_all x1, blocking collectives, local(): lax.all_to_all(results.reshape(devices, 4 * chunks, LANES), 'row', split_...  9.81 us
    ppermute x4, starting transfers between devices, local(): came.append(lax.ppermute(piece, 'row', pairs))  7.52 us
    pallas_call x1, Pallas kernels, local(): pl.pallas_call(spread_kernel, out_shape=[jax.ShapeDtypeStruct(spread_shap...  4 us
    pallas_call x1, Pallas kernels, local(): pl.pallas_call(lambda *refs: degrid_kernel(per_dest, *refs), out_shape=ja...  3.36 us
    pallas_call x1, Pallas kernels, local(): pl.pallas_call(lambda *refs: own_facet_kernel(devices, *refs), out_shape=...  1.55 us
    pallas_call x1, Pallas kernels, local(): pl.pallas_call(lambda *refs: place_kernel(devices, chunks, *refs), out_sh...  0.69 us
  transfers between devices with their start and end apart: 5, of which 0 were waited for; matrix products, arithmetic and copies ran while one was open for 0% of the time, Pallas kernels for 20%

profile of v7, /device:TPU:0, one launch (start us, length us, event | category | flops | bytes accessed | tf_op | source)
XLA Modules:
  0.0 27.8 jit_solution(4613568014138873503)
XLA Ops:
  0.0 0.5 %collective-permute-start = (bf16[2,16,32,128]{3,2,1,0:T(8,128)(2,1)}, bf16[2,16,32,128]{3,2,1,0:T(8,128)(2,1)S(1)}, u32[]{:S(2)}, u32[]{:S(2)}) collective-permute-start(bf16[2,16,32,128]{3,2,1,0:T(8,128)(2,1)} %refs_4_.1), channel_id=1, source_target_pairs={{0,1},{1,0},{2,3},{3,2},{4,5},{5,4},{6,7},{7,6},{8,9},{9,8},{10,11... | collective-permute-start | bytes 786440 | tf_op jit(solution)/shard_map/ppermute | solution.py:330
  0.5 1.5 %own_facet_sums.1 = (bf16[64,256]{1,0:T(8,128)(2,1)S(1)}, bf16[64,256]{1,0:T(8,128)(2,1)S(1)}, bf16[64,256]{1,0:T(8,128)(2,1)S(1)}, bf16[64,256]{1,0:T(8,128)(2,...) custom-call(s32[32]{0:T(128)} %refs_0_.1, ...), custom_call_target="tpu_custom_call" | custom-call | tf_op jit(solution)/shard_map/own_facet_sums/pallas_call | solution.py:334
  2.0 0.0 collective-permute-done.rows_ref
  2.0 0.3 %other_facet_sums.1 = (bf16[128,256]{1,0:T(8,128)(2,1)S(1)}, bf16[128,256]{1,0:T(8,128)(2,1)S(1)}, bf16[128,256]{1,0:T(8,128)(2,1)S(1)}, bf16[128,256]{1,0:T(8,1...) custom-call(bf16[2,16,32,128]{3,2,1,0:T(8,128)(2,1)S(1)} %collective-permute-done.rows_ref, ...), custom_call_target="tpu_custom_call" | custom-call | tf_op jit(solution)/shard_map/other_facet_sums/pallas_call | solution.py:359
  2.4 2.7 %collective-permute-start.1 = (bf16[128,256]{1,0:T(8,128)(2,1)S(1)}, bf16[128,256]{1,0:T(8,128)(2,1)S(1)}, u32[]{:S(2)}, u32[]{:S(2)}) collective-permute-start(bf16[128,256]{1,0:T(8,128)(2,1)S(1)} %get-tuple-element.34), channel_id=1, source_target_pairs={{0,5},{1,4},{2,7},{3,6},{4,9},{5,8},{6,11},{7,10},{8,13},{9,12},{1... | collective-permute-start | bytes 196616 | tf_op jit(solution)/shard_map/ppermute | solution.py:375
  5.1 3.1 %collective-permute-start.2 = (bf16[128,256]{1,0:T(8,128)(2,1)S(1)}, bf16[128,256]{1,0:T(8,128)(2,1)S(1)}, u32[]{:S(2)}, u32[]{:S(2)}) collective-permute-start(bf16[128,256]{1,0:T(8,128)(2,1)S(1)} %get-tuple-element.35), channel_id=1, source_target_pairs={{0,15},{1,14},{2,5},{3,4},{4,3},{5,2},{6,9},{7,8},{8,7},{9,6},{10,... | collective-permute-start | bytes 196616 | tf_op jit(solution)/shard_map/ppermute | solution.py:375
  8.2 1.7 %collective-permute-start.3 = (bf16[128,256]{1,0:T(8,128)(2,1)S(1)}, bf16[128,256]{1,0:T(8,128)(2,1)S(1)}, u32[]{:S(2)}, u32[]{:S(2)}) collective-permute-start(bf16[128,256]{1,0:T(8,128)(2,1)S(1)} %get-tuple-element.36), channel_id=1, source_target_pairs={{0,13},{1,12},{2,15},{3,14},{4,1},{5,0},{6,3},{7,2},{8,5},{9,4},{1... | collective-permute-start | bytes 196616 | tf_op jit(solution)/shard_map/ppermute | solution.py:375
  9.8 0.1 collective-permute-start.4
  9.9 4.0 %spread.1 = (bf16[2,256,8192]{2,1,0:T(8,128)(2,1)S(1)}, f32[2,256,8192]{2,1,0:T(8,128)S(1)}) custom-call(s32[2,8,128]{2,1,0:T(8,128)S(1)} %get-tuple-element.38.shifts_ref, f32[8,256]{1,0:T(8,128)S(1)} %get-tuple-element.39.table_ref, bf16[256,256]{1,0:T(8,128)(2,1)S(1)} %get-tuple-element.40.transform_ref, s32[2,8192]{1,0:T(2,128)S(1)} %get-tuple-element.41.row_ref, ...), custom_call_target="tpu_custom_call" | custom-call | flops 2147483648 | bytes 25165824 | tf_op jit(solution)/shard_map/spread/pallas_call | solution.py:378
  13.9 0.0 collective-permute-done.1.refs_1_
  13.9 0.0 collective-permute-done.2.refs_2_
  13.9 0.0 collective-permute-done.3.refs_3_
  13.9 0.0 collective-permute-done.4.refs_4_
  14.0 3.4 %degrid.1 = bf16[256,128]{1,0:T(8,128)(2,1)S(1)} custom-call(bf16[128,256]{1,0:T(8,128)(2,1)S(1)} %get-tuple-element.33.refs_0_, bf16[128,256]{1,0:T(8,128)(2,1)S(1)} %collective-permute-done.1.refs_1_, bf16[128,256]{1,0:T(8,128)(2,1)S(1)} %collective-permute-done.2.refs_2_, bf16[128,256]{1,0:T(8,128)(2,1)S(1)} %collective-permute-done.3.refs_3_, ...), custom_call_target="tpu_custom_call" | custom-call | tf_op jit(solution)/shard_map/degrid/pallas_call | solution.py:392
  17.3 9.8 %all_to_all.5 = bf16[16,16,128]{2,1,0:T(8,128)(2,1)S(1)} all-to-all(bf16[16,16,128]{2,1,0:T(8,128)(2,1)S(1)} %bitcast.4), channel_id=1, replica_groups=mesh['grp'=2,'row'=16] {'row'}, dimensions={0} | all-to-all | bytes 131072 | tf_op jit(solution)/shard_map/all_to_all | solution.py:404
  27.1 0.7 %place.1 = f32[2,32,512]{2,1,0:T(8,128)} custom-call(bf16[256,128]{1,0:T(8,128)(2,1)S(1)} %bitcast.5), custom_call_target="tpu_custom_call" | custom-call | tf_op jit(solution)/shard_map/place/pallas_call | solution.py:407
Async XLA Ops:
  0.0 2.0 %collective-permute-start = (bf16[2,16,32,128]{3,2,1,0:T(8,128)(2,1)}, bf16[2,16,32,128]{3,2,1,0:T(8,128)(2,1)S(1)}, u32[]{:S(2)}, u32[]{:S(2)}) collective-permute-start(bf16[2,16,32,128]{3,2,1,0:T(8,128)(2,1)} %refs_4_.1), channel_id=1, source_target_pairs={{0,1},{1,0},{2,3},{3,2},{4,5},{5,4},{6,7},{7,6},{8,9},{9,8},{10,11... | collective-permute-start | bytes 786440 | tf_op jit(solution)/shard_map/ppermute | solution.py:330
  2.4 11.5 %collective-permute-start.1 = (bf16[128,256]{1,0:T(8,128)(2,1)S(1)}, bf16[128,256]{1,0:T(8,128)(2,1)S(1)}, u32[]{:S(2)}, u32[]{:S(2)}) collective-permute-start(bf16[128,256]{1,0:T(8,128)(2,1)S(1)} %get-tuple-element.34), channel_id=1, source_target_pairs={{0,5},{1,4},{2,7},{3,6},{4,9},{5,8},{6,11},{7,10},{8,13},{9,12},{1... | collective-permute-start | bytes 196616 | tf_op jit(solution)/shard_map/ppermute | solution.py:375
  5.1 8.8 %collective-permute-start.2 = (bf16[128,256]{1,0:T(8,128)(2,1)S(1)}, bf16[128,256]{1,0:T(8,128)(2,1)S(1)}, u32[]{:S(2)}, u32[]{:S(2)}) collective-permute-start(bf16[128,256]{1,0:T(8,128)(2,1)S(1)} %get-tuple-element.35), channel_id=1, source_target_pairs={{0,15},{1,14},{2,5},{3,4},{4,3},{5,2},{6,9},{7,8},{8,7},{9,6},{10,... | collective-permute-start | bytes 196616 | tf_op jit(solution)/shard_map/ppermute | solution.py:375
  8.2 5.8 %collective-permute-start.3 = (bf16[128,256]{1,0:T(8,128)(2,1)S(1)}, bf16[128,256]{1,0:T(8,128)(2,1)S(1)}, u32[]{:S(2)}, u32[]{:S(2)}) collective-permute-start(bf16[128,256]{1,0:T(8,128)(2,1)S(1)} %get-tuple-element.36), channel_id=1, source_target_pairs={{0,13},{1,12},{2,15},{3,14},{4,1},{5,0},{6,3},{7,2},{8,5},{9,4},{1... | collective-permute-start | bytes 196616 | tf_op jit(solution)/shard_map/ppermute | solution.py:375
  9.8 4.1 %collective-permute-start.4 = (bf16[128,256]{1,0:T(8,128)(2,1)S(1)}, bf16[128,256]{1,0:T(8,128)(2,1)S(1)}, u32[]{:S(2)}, u32[]{:S(2)}) collective-permute-start(bf16[128,256]{1,0:T(8,128)(2,1)S(1)} %get-tuple-element.37), channel_id=1, source_target_pairs={{0,3},{1,2},{2,1},{3,0},{4,7},{5,6},{6,5},{7,4},{8,11},{9,10},{10,... | collective-permute-start | bytes 196616 | tf_op jit(solution)/shard_map/ppermute | solution.py:375

commit v8 on v7

--- a/solution.py
+++ b/solution.py
@@ -278,7 +278,7 @@
         lanes = pl.ds(pl.multiple_of(block * PART, PART), PART)
         for sub in range(SUB_DEV):
             along = jnp.dot(waves[sub], row_spread[sub, :, lanes], preferred_element_type=jnp.float32)
-            sums = [None, None]
+            halves = [[None, None], [None, None]]
             for t in range(KC // 8):
                 real = slice(16 * t, 16 * t + 8)
                 imag = slice(16 * t + 8, 16 * t + 16)
@@ -288,7 +288,8 @@
                     along[real] * real_wave - along[imag] * imag_wave,
                     along[real] * imag_wave + along[imag] * real_wave,
                 )
-                sums = [term if t == 0 else total + term for total, term in zip(sums, terms)]
+                halves[t % 2] = [term if t < 2 else total + term for total, term in zip(halves[t % 2], terms)]
+            sums = [first_half + second_half for first_half, second_half in zip(*halves)]
             first = block * (PART // LANES * 4)
             for part in range(2):
                 total = jnp.sum(sums[part], axis=0, keepdims=True)

time: 28 us -> 28.1 us (level)
  no operation moved by 1% of the time
where the time goes in v8:
time: 28.1 us; the launch traced here: 27.9 us
  Pallas kernels  10 us (36%)
  blocking collectives  9.81 us (35%)
  starting transfers between devices  7.98 us (28%)
    all_to_all x1, blocking collectives, local(): lax.all_to_all(results.reshape(devices, 4 * chunks, LANES), 'row', split_...  9.81 us
    ppermute x4, starting transfers between devices, local(): came.append(lax.ppermute(piece, 'row', pairs))  7.53 us
    pallas_call x1, Pallas kernels, local(): pl.pallas_call(spread_kernel, out_shape=[jax.ShapeDtypeStruct(spread_shap...  4 us
    pallas_call x1, Pallas kernels, local(): pl.pallas_call(lambda *refs: degrid_kernel(per_dest, *refs), out_shape=ja...  3.41 us
    pallas_call x1, Pallas kernels, local(): pl.pallas_call(lambda *refs: own_facet_kernel(devices, *refs), out_shape=...  1.55 us
    pallas_call x1, Pallas kernels, local(): pl.pallas_call(lambda *refs: place_kernel(devices, chunks, *refs), out_sh...  0.69 us
  transfers between devices with their start and end apart: 5, of which 0 were waited for; matrix products, arithmetic and copies ran while one was open for 0% of the time, Pallas kernels for 20%

profile of v8, /device:TPU:0, one launch (start us, length us, event | category | flops | bytes accessed | tf_op | source)
XLA Modules:
  0.0 27.9 jit_solution(15567617414245056054)
XLA Ops:
  0.0 0.5 %collective-permute-start = (bf16[2,16,32,128]{3,2,1,0:T(8,128)(2,1)}, bf16[2,16,32,128]{3,2,1,0:T(8,128)(2,1)S(1)}, u32[]{:S(2)}, u32[]{:S(2)}) collective-permute-start(bf16[2,16,32,128]{3,2,1,0:T(8,128)(2,1)} %refs_4_.1), channel_id=1, source_target_pairs={{0,1},{1,0},{2,3},{3,2},{4,5},{5,4},{6,7},{7,6},{8,9},{9,8},{10,11... | collective-permute-start | bytes 786440 | tf_op jit(solution)/shard_map/ppermute | solution.py:331
  0.5 1.6 %own_facet_sums.1 = (bf16[64,256]{1,0:T(8,128)(2,1)S(1)}, bf16[64,256]{1,0:T(8,128)(2,1)S(1)}, bf16[64,256]{1,0:T(8,128)(2,1)S(1)}, bf16[64,256]{1,0:T(8,128)(2,...) custom-call(s32[32]{0:T(128)} %refs_0_.1, ...), custom_call_target="tpu_custom_call" | custom-call | tf_op jit(solution)/shard_map/own_facet_sums/pallas_call | solution.py:335
  2.0 0.0 collective-permute-done.rows_ref
  2.0 0.3 %other_facet_sums.1 = (bf16[128,256]{1,0:T(8,128)(2,1)S(1)}, bf16[128,256]{1,0:T(8,128)(2,1)S(1)}, bf16[128,256]{1,0:T(8,128)(2,1)S(1)}, bf16[128,256]{1,0:T(8,1...) custom-call(bf16[2,16,32,128]{3,2,1,0:T(8,128)(2,1)S(1)} %collective-permute-done.rows_ref, ...), custom_call_target="tpu_custom_call" | custom-call | tf_op jit(solution)/shard_map/other_facet_sums/pallas_call | solution.py:360
  2.4 2.7 %collective-permute-start.1 = (bf16[128,256]{1,0:T(8,128)(2,1)S(1)}, bf16[128,256]{1,0:T(8,128)(2,1)S(1)}, u32[]{:S(2)}, u32[]{:S(2)}) collective-permute-start(bf16[128,256]{1,0:T(8,128)(2,1)S(1)} %get-tuple-element.34), channel_id=1, source_target_pairs={{0,5},{1,4},{2,7},{3,6},{4,9},{5,8},{6,11},{7,10},{8,13},{9,12},{1... | collective-permute-start | bytes 196616 | tf_op jit(solution)/shard_map/ppermute | solution.py:376
  5.1 3.1 %collective-permute-start.2 = (bf16[128,256]{1,0:T(8,128)(2,1)S(1)}, bf16[128,256]{1,0:T(8,128)(2,1)S(1)}, u32[]{:S(2)}, u32[]{:S(2)}) collective-permute-start(bf16[128,256]{1,0:T(8,128)(2,1)S(1)} %get-tuple-element.35), channel_id=1, source_target_pairs={{0,15},{1,14},{2,5},{3,4},{4,3},{5,2},{6,9},{7,8},{8,7},{9,6},{10,... | collective-permute-start | bytes 196616 | tf_op jit(solution)/shard_map/ppermute | solution.py:376
  8.2 1.7 %collective-permute-start.3 = (bf16[128,256]{1,0:T(8,128)(2,1)S(1)}, bf16[128,256]{1,0:T(8,128)(2,1)S(1)}, u32[]{:S(2)}, u32[]{:S(2)}) collective-permute-start(bf16[128,256]{1,0:T(8,128)(2,1)S(1)} %get-tuple-element.36), channel_id=1, source_target_pairs={{0,13},{1,12},{2,15},{3,14},{4,1},{5,0},{6,3},{7,2},{8,5},{9,4},{1... | collective-permute-start | bytes 196616 | tf_op jit(solution)/shard_map/ppermute | solution.py:376
  9.8 0.1 collective-permute-start.4
  9.9 4.0 %spread.1 = (bf16[2,256,8192]{2,1,0:T(8,128)(2,1)S(1)}, f32[2,256,8192]{2,1,0:T(8,128)S(1)}) custom-call(s32[2,8,128]{2,1,0:T(8,128)S(1)} %get-tuple-element.38.shifts_ref, f32[8,256]{1,0:T(8,128)S(1)} %get-tuple-element.39.table_ref, bf16[256,256]{1,0:T(8,128)(2,1)S(1)} %get-tuple-element.40.transform_ref, s32[2,8192]{1,0:T(2,128)S(1)} %get-tuple-element.41.row_ref, ...), custom_call_target="tpu_custom_call" | custom-call | flops 2147483648 | bytes 25165824 | tf_op jit(solution)/shard_map/spread/pallas_call | solution.py:379
  13.9 0.0 collective-permute-done.1.refs_1_
  13.9 0.0 collective-permute-done.2.refs_2_
  13.9 0.0 collective-permute-done.3.refs_3_
  13.9 0.0 collective-permute-done.4.refs_4_
  14.0 3.4 %degrid.1 = bf16[256,128]{1,0:T(8,128)(2,1)S(1)} custom-call(bf16[128,256]{1,0:T(8,128)(2,1)S(1)} %get-tuple-element.33.refs_0_, bf16[128,256]{1,0:T(8,128)(2,1)S(1)} %collective-permute-done.1.refs_1_, bf16[128,256]{1,0:T(8,128)(2,1)S(1)} %collective-permute-done.2.refs_2_, bf16[128,256]{1,0:T(8,128)(2,1)S(1)} %collective-permute-done.3.refs_3_, ...), custom_call_target="tpu_custom_call" | custom-call | tf_op jit(solution)/shard_map/degrid/pallas_call | solution.py:393
  17.4 9.8 %all_to_all.5 = bf16[16,16,128]{2,1,0:T(8,128)(2,1)S(1)} all-to-all(bf16[16,16,128]{2,1,0:T(8,128)(2,1)S(1)} %bitcast.4), channel_id=1, replica_groups=mesh['grp'=2,'row'=16] {'row'}, dimensions={0} | all-to-all | bytes 131072 | tf_op jit(solution)/shard_map/all_to_all | solution.py:405
  27.2 0.7 %place.1 = f32[2,32,512]{2,1,0:T(8,128)} custom-call(bf16[256,128]{1,0:T(8,128)(2,1)S(1)} %bitcast.5), custom_call_target="tpu_custom_call" | custom-call | tf_op jit(solution)/shard_map/place/pallas_call | solution.py:408
Async XLA Ops:
  0.0 2.0 %collective-permute-start = (bf16[2,16,32,128]{3,2,1,0:T(8,128)(2,1)}, bf16[2,16,32,128]{3,2,1,0:T(8,128)(2,1)S(1)}, u32[]{:S(2)}, u32[]{:S(2)}) collective-permute-start(bf16[2,16,32,128]{3,2,1,0:T(8,128)(2,1)} %refs_4_.1), channel_id=1, source_target_pairs={{0,1},{1,0},{2,3},{3,2},{4,5},{5,4},{6,7},{7,6},{8,9},{9,8},{10,11... | collective-permute-start | bytes 786440 | tf_op jit(solution)/shard_map/ppermute | solution.py:331
  2.4 11.5 %collective-permute-start.1 = (bf16[128,256]{1,0:T(8,128)(2,1)S(1)}, bf16[128,256]{1,0:T(8,128)(2,1)S(1)}, u32[]{:S(2)}, u32[]{:S(2)}) collective-permute-start(bf16[128,256]{1,0:T(8,128)(2,1)S(1)} %get-tuple-element.34), channel_id=1, source_target_pairs={{0,5},{1,4},{2,7},{3,6},{4,9},{5,8},{6,11},{7,10},{8,13},{9,12},{1... | collective-permute-start | bytes 196616 | tf_op jit(solution)/shard_map/ppermute | solution.py:376
  5.1 8.8 %collective-permute-start.2 = (bf16[128,256]{1,0:T(8,128)(2,1)S(1)}, bf16[128,256]{1,0:T(8,128)(2,1)S(1)}, u32[]{:S(2)}, u32[]{:S(2)}) collective-permute-start(bf16[128,256]{1,0:T(8,128)(2,1)S(1)} %get-tuple-element.35), channel_id=1, source_target_pairs={{0,15},{1,14},{2,5},{3,4},{4,3},{5,2},{6,9},{7,8},{8,7},{9,6},{10,... | collective-permute-start | bytes 196616 | tf_op jit(solution)/shard_map/ppermute | solution.py:376
  8.2 5.8 %collective-permute-start.3 = (bf16[128,256]{1,0:T(8,128)(2,1)S(1)}, bf16[128,256]{1,0:T(8,128)(2,1)S(1)}, u32[]{:S(2)}, u32[]{:S(2)}) collective-permute-start(bf16[128,256]{1,0:T(8,128)(2,1)S(1)} %get-tuple-element.36), channel_id=1, source_target_pairs={{0,13},{1,12},{2,15},{3,14},{4,1},{5,0},{6,3},{7,2},{8,5},{9,4},{1... | collective-permute-start | bytes 196616 | tf_op jit(solution)/shard_map/ppermute | solution.py:376
  9.8 4.1 %collective-permute-start.4 = (bf16[128,256]{1,0:T(8,128)(2,1)S(1)}, bf16[128,256]{1,0:T(8,128)(2,1)S(1)}, u32[]{:S(2)}, u32[]{:S(2)}) collective-permute-start(bf16[128,256]{1,0:T(8,128)(2,1)S(1)} %get-tuple-element.37), channel_id=1, source_target_pairs={{0,3},{1,2},{2,1},{3,0},{4,7},{5,6},{6,5},{7,4},{8,11},{9,10},{10,... | collective-permute-start | bytes 196616 | tf_op jit(solution)/shard_map/ppermute | solution.py:376
